TPU v7x, 512 devices: a whole 4x8x8 slice. The times are simulated.
512 devices in a mesh: gx: 64 (over x, z, core), gy: 8 (over y).
Axes of the slice: x: 4, y: 8, z: 8, core: 2. Of those that a mesh axis runs over, the one named last changes fastest.
Arguments:
- source: float32 [1024, 256, 128], P('gx', 'gy'), may hold values from -6 to 6
- tissue: int32 [1024, 256, 128], P('gx', 'gy'), may hold values from 0 to 7
- diffusivity: float32 [8], replicated, may hold values from 0.2 to 5
- uptake: float32 [8], replicated, may hold values from 0.002 to 0.05
Outputs:
- ligand: float32 [1024, 256, 128], P('gx', 'gy')
All inputs are finite; a program needn't handle non-finite values.
Results may differ from a plain program's by a relative error of at most 0.00002.
Values sent between devices are 32-bit elements; how exact they have to be, the bound alone decides.
A program may use at most 64 MiB of HBM per device.

v0:
```python
import jax
import jax.numpy as jnp
from jax import lax
from jax.sharding import PartitionSpec as P

LEVELS = 6
COARSE = 4


OMEGA = 0.8
ZFACE = 0.015625


def extended(shard, sides, width):
    for axis, dim in sides:
        devices, length = (lax.axis_size(axis), shard.shape[dim])
        up = [(i, (i + 1) % devices) for i in range(devices - 1)]
        down = [(j, i) for i, j in up]
        last = lax.slice_in_dim(shard, length - width, length, axis=dim)
        initial = lax.slice_in_dim(shard, 0, width, axis=dim)
        before = lax.ppermute(last, axis, up)
        after = lax.ppermute(initial, axis, down)
        shard = jnp.concatenate([before, shard, after], axis=dim)
    return shard


def shifted(value, axis, steps):
    count = lax.axis_size(axis)
    initial, last = (max(0, -steps), min(count, count - steps))
    return lax.ppermute(value, axis, [(source, source + steps) for source in range(initial, last)])


def from_partner(shard, axis, apart):
    return lax.ppermute(shard, axis, [(i, i ^ 1 << apart) for i in range(lax.axis_size(axis))])


def operate(u_pad, kap_pad, sig, scale):
    kc = kap_pad[1:-1, 1:-1]
    core = u_pad[1:-1, 1:-1]
    east = 0.5 * scale * (kc + kap_pad[2:, 1:-1])
    west = 0.5 * scale * (kc + kap_pad[:-2, 1:-1])
    north = 0.5 * scale * (kc + kap_pad[1:-1, 2:])
    south = 0.5 * scale * (kc + kap_pad[1:-1, :-2])
    kap_z = jnp.pad(kc, ((0, 0), (0, 0), (1, 1)))
    upper = 0.5 * ZFACE * (kc + kap_z[:, :, 2:])
    lower = 0.5 * ZFACE * (kc + kap_z[:, :, :-2])
    core_z = jnp.pad(core, ((0, 0), (0, 0), (1, 1)))
    diag = east + west + north + south + upper + lower + sig
    pulled = (
        east * u_pad[2:, 1:-1]
        + west * u_pad[:-2, 1:-1]
        + north * u_pad[1:-1, 2:]
        + south * u_pad[1:-1, :-2]
        + upper * core_z[:, :, 2:]
        + lower * core_z[:, :, :-2]
    )
    return (diag, diag * core - pulled)


def relax(u_pad, rhs, kap_pad, sig, scale):
    diag, applied = operate(u_pad, kap_pad, sig, scale)
    core = u_pad[1:-1, 1:-1]
    return core + OMEGA * (rhs - applied) / diag


def restrict(field):
    return 0.25 * (field[0::2, 0::2] + field[1::2, 0::2] + (field[0::2, 1::2] + field[1::2, 1::2]))


def prolong(field):
    return jnp.repeat(jnp.repeat(field, 2, axis=0), 2, axis=1)


def blank(field):
    return jnp.zeros((field.shape[0] + 2, field.shape[1] + 2, field.shape[2]), jnp.float32)


def grid_rims(field):
    return extended(field, (("gx", 0), ("gy", 1)), 1)


def plane_rims(field):
    return extended(field, (("gy", 1),), 1)


def fold_rims(field, step):
    middle = plane_rims(field)
    below = shifted(field[-1:], "gx", step)
    above = shifted(field[:1], "gx", -step)
    below = jnp.pad(below, ((0, 0), (1, 1), (0, 0)))
    above = jnp.pad(above, ((0, 0), (1, 1), (0, 0)))
    return jnp.concatenate([below, middle, above], axis=0)


def fold_in(pack, bit):
    other = from_partner(pack, "gx", bit)
    first = lax.axis_index("gx") // 2**bit % 2 == 0
    leading = jnp.where(first, pack, other)
    trailing = jnp.where(first, other, pack)
    return jnp.concatenate([leading, trailing], axis=1)


def own_row(field, bit):
    position = lax.axis_index("gx") // 2**bit % 2
    return lax.dynamic_slice_in_dim(field, position, 1, 0)


def plain_down(rhs, kappa, sigma, scale):
    kap_pad = grid_rims(kappa)
    smooth = relax(blank(rhs), rhs, kap_pad, sigma, scale)
    smooth = relax(grid_rims(smooth), rhs, kap_pad, sigma, scale)
    diag, applied = operate(grid_rims(smooth), kap_pad, sigma, scale)
    return (smooth, rhs - applied, ("plain", rhs, kap_pad, sigma))


def plain_up(field, record, scale):
    rhs, kap_pad, sigma = (record[1], record[2], record[3])
    for turn in range(2):
        field = relax(grid_rims(field), rhs, kap_pad, sigma, scale)
    return field


def coarse_pair(pack, edge_three, edge_four, lift, lower_four, lower_three):
    kappa, sigma, rhs = (pack[0], pack[1], pack[2])
    scale = 0.25 ** (LEVELS - 2)
    kap_pad = edge_three(kappa)
    smooth = relax(blank(rhs), rhs, kap_pad, sigma, scale)
    smooth = relax(edge_three(smooth), rhs, kap_pad, sigma, scale)
    diag, applied = operate(edge_three(smooth), kap_pad, sigma, scale)
    four = lift(jnp.stack([restrict(kappa), restrict(sigma), restrict(rhs - applied)]))
    scale_four = 0.25 ** (LEVELS - 1)
    kap_four = edge_four(four[0])
    coarsest = relax(blank(four[2]), four[2], kap_four, four[1], scale_four)
    for turn in range(COARSE - 1):
        coarsest = relax(edge_four(coarsest), four[2], kap_four, four[1], scale_four)
    field = smooth + prolong(lower_four(coarsest))
    for turn in range(2):
        field = relax(edge_three(field), rhs, kap_pad, sigma, scale)
    return lower_three(field)


def body(source, tissue, diffusivity, uptake):
    kappa = jnp.zeros(tissue.shape, jnp.float32)
    sigma = jnp.zeros(tissue.shape, jnp.float32)
    for kind in range(diffusivity.shape[0]):
        hit = tissue == kind
        kappa = jnp.where(hit, diffusivity[kind], kappa)
        sigma = jnp.where(hit, uptake[kind], sigma)
    rhs = source
    records = []
    for level in range(LEVELS - 2):
        scale = 0.25**level
        smooth, residual, record = plain_down(rhs, kappa, sigma, scale)
        records.append((smooth, record))
        rhs = restrict(residual)
        kappa = restrict(kappa)
        sigma = restrict(sigma)
    pack = jnp.stack([kappa, sigma, rhs])

    def edge_near(field):
        return fold_rims(field, 2)

    def edge_far(field):
        return fold_rims(field, 4)

    def lift_far(value):
        return fold_in(value, 1)

    def row_far(field):
        return own_row(field, 1)

    def row_near(field):
        return own_row(field, 0)

    correction = coarse_pair(fold_in(pack, 0), edge_near, edge_far, lift_far, row_far, row_near)
    for level in reversed(range(LEVELS - 2)):
        scale = 0.25**level
        smooth, record = records[level]
        field = smooth + prolong(correction)
        correction = plain_up(field, record, scale)
    return correction


def solution(mesh):
    in_specs = (P("gx", "gy", None), P("gx", "gy", None), P(), P())
    out_specs = P("gx", "gy", None)
    return jax.shard_map(body, mesh=mesh, in_specs=in_specs, out_specs=out_specs, check_vma=False)
```

profile of v0, /device:TPU:62, one launch (start us, length us, event | category | flops | bytes accessed | tf_op | source)
XLA Modules:
  0.0 529.4 jit_solution(6480699755329184332)
XLA Ops:
  1.6 6.4 %select_select_fusion.1 = (f32[16,32,128]{2,1,0:T(8,128)S(1)}, pred[16,32,128]{2,1,0:T(8,128)(4,1)S(1)}, pred[16,32,128]{2,1,0:T(8,128)(4,1)S(1)}, pred[16,32,12...) fusion(f32[]{:T(128)} %bitcast.7, f32[]{:T(128)} %bitcast.6, ...), kind=kLoop, calls=%fused_computation.132 | loop fusion | flops 1048576 | bytes 1048608 | tf_op jit(solution)/shard_map/jit(_where)/select_n | solution.py:147
  8.0 10.7 %collective-permute-start = (f32[1,32,128]{2,1,0:T(8,128)S(1)}, f32[1,32,128]{2,1,0:T(8,128)S(1)}, u32[]{:S(2)}, u32[]{:S(2)}) collective-permute-start(f32[1,32,128]{2,1,0:T(8,128)S(1)} %get-tuple-element.73), channel_id=1, source_target_pairs={{8,0},{16,8},{24,16},{32,24},{40,32},{48,40},{56,48},{64,56},{72,6... | collective-permute-start | bytes 49160 | tf_op jit(solution)/shard_map/ppermute | solution.py:22
  20.8 5.2 collective-permute-done.1
  34.9 5.6 %fusion.43 = (f32[16,32,128]{2,1,0:T(8,128)S(1)}, f32[16,32,128]{2,1,0:T(8,128)S(1)}, f32[16,32,128]{2,1,0:T(8,128)S(1)}, f32[16,32,128]{2,1,0:T(8,128)S(1)}) fusion(f32[16,32,128]{2,1,0:T(8,128)S(1)} %copy-done, f32[16,32,128]{2,1,0:T(8,128)S(1)} %broadcast.227, f32[16,32,128]{2,1,0:T(8,128)S(1)} %get-tuple-element.45, ...), kind=kLoop, calls=%fused_computation.55 | loop fusion | flops 3080192 | bytes 2410528 | tf_op jit(solution)/shard_map/div | solution.py:63
  54.2 4.2 collective-permute-done.7
  63.2 5.3 collective-permute-start.12
  91.6 4.6 collective-permute-done.17
  101.1 4.2 collective-permute-done.19
  109.8 5.3 collective-permute-start.24
  122.2 4.6 collective-permute-start.26
  133.2 4.3 collective-permute-start.28
  139.8 4.7 collective-permute-done.29
  158.1 5.3 collective-permute-start.36
  165.4 4.3 collective-permute-start.34
  171.0 4.6 collective-permute-start.38
  187.3 5.1 collective-permute-done.41
  206.0 4.5 collective-permute-done.45
  210.5 4.3 collective-permute-start.46
  224.9 4.5 collective-permute-start.50
  240.4 4.6 collective-permute-start.54
  255.9 4.6 collective-permute-start.58
  276.9 4.6 collective-permute-start.63
  283.4 4.8 collective-permute-start.65
  293.2 5.6 %collective-permute-start.67 = (f32[2,1,128]{2,0,1:T(2,128)S(1)}, f32[2,1,128]{2,0,1:T(2,128)S(1)}, u32[]{:S(2)}, u32[]{:S(2)}) collective-permute-start(f32[2,1,128]{2,0,1:T(2,128)S(1)} %get-tuple-element.13), channel_id=1, source_target_pairs={{1,0},{2,1},{3,2},{4,3},{5,4},{6,5},{7,6},{9,8},{10,9},{11,10},{12... | collective-permute-start | bytes 3080 | tf_op jit(solution)/shard_map/ppermute | solution.py:22
  300.8 4.8 collective-permute-start.69
  310.6 5.8 %collective-permute-start.71 = (f32[2,1,128]{2,0,1:T(2,128)S(1)}, f32[2,1,128]{2,0,1:T(2,128)S(1)}, u32[]{:S(2)}, u32[]{:S(2)}) collective-permute-start(f32[2,1,128]{2,0,1:T(2,128)S(1)} %divide_add_fusion.4), channel_id=1, source_target_pairs={{1,0},{2,1},{3,2},{4,3},{5,4},{6,5},{7,6},{9,8},{10,9},{11,10},{12... | collective-permute-start | bytes 3080 | tf_op jit(solution)/shard_map/ppermute | solution.py:22
  318.7 4.4 collective-permute-start.73
  328.6 5.8 %collective-permute-start.75 = (f32[2,1,128]{2,0,1:T(2,128)S(1)}, f32[2,1,128]{2,0,1:T(2,128)S(1)}, u32[]{:S(2)}, u32[]{:S(2)}) collective-permute-start(f32[2,1,128]{2,0,1:T(2,128)S(1)} %divide_add_fusion.3), channel_id=1, source_target_pairs={{1,0},{2,1},{3,2},{4,3},{5,4},{6,5},{7,6},{9,8},{10,9},{11,10},{12... | collective-permute-start | bytes 3080 | tf_op jit(solution)/shard_map/ppermute | solution.py:22
  341.1 5.0 collective-permute-done.77
  347.6 5.8 %collective-permute-start.79 = (f32[2,1,128]{2,1,0:T(1,128)S(1)}, f32[2,1,128]{2,1,0:T(1,128)S(1)}, u32[]{:S(2)}, u32[]{:S(2)}) collective-permute-start(f32[2,1,128]{2,1,0:T(1,128)S(1)} %get-tuple-element.144), channel_id=1, source_target_pairs={{1,0},{2,1},{3,2},{4,3},{5,4},{6,5},{7,6},{9,8},{10,9},{11,10},{12... | collective-permute-start | bytes 3080 | tf_op jit(solution)/shard_map/ppermute | solution.py:22
  364.3 5.8 %collective-permute-start.83 = (f32[2,1,128]{2,1,0:T(1,128)S(1)}, f32[2,1,128]{2,1,0:T(1,128)S(1)}, u32[]{:S(2)}, u32[]{:S(2)}) collective-permute-start(f32[2,1,128]{2,1,0:T(1,128)S(1)} %get-tuple-element.140), channel_id=1, source_target_pairs={{1,0},{2,1},{3,2},{4,3},{5,4},{6,5},{7,6},{9,8},{10,9},{11,10},{12... | collective-permute-start | bytes 3080 | tf_op jit(solution)/shard_map/ppermute | solution.py:22
  384.0 4.6 collective-permute-done.87
  388.6 5.1 collective-permute-start.88
  395.1 5.4 %collective-permute-done.89 = f32[4,1,128]{2,1,0:T(1,128)S(1)} collective-permute-done((f32[4,1,128]{2,1,0:T(1,128)S(1)}, f32[4,1,128]{2,1,0:T(1,128)S(1)}, u32[]{:S(2)}, u32[]{:S(2)}) %collective-permute-start.89) | collective-permute-done | bytes 2080 | tf_op jit(solution)/shard_map/ppermute | solution.py:21
  404.9 4.6 collective-permute-done.91
  409.5 5.1 collective-permute-start.92
  424.6 4.6 collective-permute-done.95
  434.4 4.2 collective-permute-done.97
  443.0 4.6 collective-permute-done.99
  452.1 4.2 collective-permute-done.101
  460.8 4.7 collective-permute-done.103
  469.9 4.2 collective-permute-done.105
  478.6 4.7 collective-permute-done.107
  487.7 4.2 collective-permute-done.109
  496.6 4.7 collective-permute-done.111
  505.8 4.2 collective-permute-done.113
  514.8 4.7 collective-permute-done.115
  524.1 4.2 collective-permute-done.117
  (368 shorter events, 290.2 us)
Async XLA Ops:
  8.0 12.7 %collective-permute-start = (f32[1,32,128]{2,1,0:T(8,128)S(1)}, f32[1,32,128]{2,1,0:T(8,128)S(1)}, u32[]{:S(2)}, u32[]{:S(2)}) collective-permute-start(f32[1,32,128]{2,1,0:T(8,128)S(1)} %get-tuple-element.73), channel_id=1, source_target_pairs={{8,0},{16,8},{24,16},{32,24},{40,32},{48,40},{56,48},{64,56},{72,6... | collective-permute-start | bytes 49160 | tf_op jit(solution)/shard_map/ppermute | solution.py:22
  18.7 7.3 %collective-permute-start.1 = (f32[1,32,128]{2,1,0:T(8,128)S(1)}, f32[1,32,128]{2,1,0:T(8,128)S(1)}, u32[]{:S(2)}, u32[]{:S(2)}) collective-permute-start(f32[1,32,128]{2,1,0:T(8,128)S(1)} %get-tuple-element.72), channel_id=1, source_target_pairs={{0,8},{8,16},{16,24},{24,32},{32,40},{40,48},{48,56},{56,64},{64,7... | collective-permute-start | bytes 49160 | tf_op jit(solution)/shard_map/ppermute | solution.py:21
  42.4 7.2 %collective-permute-start.5 = (f32[1,32,128]{2,1,0:T(8,128)S(1)}, f32[1,32,128]{2,1,0:T(8,128)S(1)}, u32[]{:S(2)}, u32[]{:S(2)}) collective-permute-start(f32[1,32,128]{2,1,0:T(8,128)S(1)} %get-tuple-element.70), channel_id=1, source_target_pairs={{0,8},{8,16},{16,24},{24,32},{32,40},{40,48},{48,56},{56,64},{64,7... | collective-permute-start | bytes 49160 | tf_op jit(solution)/shard_map/ppermute | solution.py:21
  58.9 11.6 %collective-permute-start.8 = (f32[1,32,128]{2,1,0:T(8,128)S(1)}, f32[1,32,128]{2,1,0:T(8,128)S(1)}, u32[]{:S(2)}, u32[]{:S(2)}) collective-permute-start(f32[1,32,128]{2,1,0:T(8,128)S(1)} %get-tuple-element.69), channel_id=1, source_target_pairs={{8,0},{16,8},{24,16},{32,24},{40,32},{48,40},{56,48},{64,56},{72,6... | collective-permute-start | bytes 49160 | tf_op jit(solution)/shard_map/ppermute | solution.py:22
  60.8 9.6 %collective-permute-start.9 = (f32[1,32,128]{2,1,0:T(8,128)S(1)}, f32[1,32,128]{2,1,0:T(8,128)S(1)}, u32[]{:S(2)}, u32[]{:S(2)}) collective-permute-start(f32[1,32,128]{2,1,0:T(8,128)S(1)} %get-tuple-element.68), channel_id=1, source_target_pairs={{0,8},{8,16},{16,24},{24,32},{32,40},{40,48},{48,56},{56,64},{64,7... | collective-permute-start | bytes 49160 | tf_op jit(solution)/shard_map/ppermute | solution.py:21
  63.2 11.8 %collective-permute-start.12 = (f32[1,16,128]{2,1,0:T(8,128)S(1)}, f32[1,16,128]{2,1,0:T(8,128)S(1)}, u32[]{:S(2)}, u32[]{:S(2)}) collective-permute-start(f32[1,16,128]{2,1,0:T(8,128)S(1)} %get-tuple-element.93), channel_id=1, source_target_pairs={{8,0},{16,8},{24,16},{32,24},{40,32},{48,40},{56,48},{64,56},{72,6... | collective-permute-start | bytes 24584 | tf_op jit(solution)/shard_map/ppermute | solution.py:22
  70.5 11.4 %collective-permute-start.10 = (f32[18,1,128]{2,1,0:T(1,128)S(1)}, f32[18,1,128]{2,1,0:T(1,128)S(1)}, u32[]{:S(2)}, u32[]{:S(2)}) collective-permute-start(f32[18,1,128]{2,1,0:T(1,128)S(1)} %get-tuple-element.58), channel_id=1, source_target_pairs={{1,0},{2,1},{3,2},{4,3},{5,4},{6,5},{7,6},{9,8},{10,9},{11,10},{12... | collective-permute-start | bytes 27656 | tf_op jit(solution)/shard_map/ppermute | solution.py:22
  73.7 8.2 %collective-permute-start.11 = (f32[18,1,128]{2,1,0:T(1,128)S(1)}, f32[18,1,128]{2,1,0:T(1,128)S(1)}, u32[]{:S(2)}, u32[]{:S(2)}) collective-permute-start(f32[18,1,128]{2,1,0:T(1,128)S(1)} %get-tuple-element.59), channel_id=1, source_target_pairs={{0,1},{1,2},{2,3},{3,4},{4,5},{5,6},{6,7},{8,9},{9,10},{10,11},{11... | collective-permute-start | bytes 27656 | tf_op jit(solution)/shard_map/ppermute | solution.py:21
  75.6 7.7 %collective-permute-start.14 = (f32[10,1,128]{2,1,0:T(1,128)S(1)}, f32[10,1,128]{2,1,0:T(1,128)S(1)}, u32[]{:S(2)}, u32[]{:S(2)}) collective-permute-start(f32[10,1,128]{2,1,0:T(1,128)S(1)} %get-tuple-element.83), channel_id=1, source_target_pairs={{1,0},{2,1},{3,2},{4,3},{5,4},{6,5},{7,6},{9,8},{10,9},{11,10},{12... | collective-permute-start | bytes 15368 | tf_op jit(solution)/shard_map/ppermute | solution.py:22
  105.4 11.6 %collective-permute-start.20 = (f32[1,16,128]{2,1,0:T(8,128)S(1)}, f32[1,16,128]{2,1,0:T(8,128)S(1)}, u32[]{:S(2)}, u32[]{:S(2)}) collective-permute-start(f32[1,16,128]{2,1,0:T(8,128)S(1)} %get-tuple-element.89), channel_id=1, source_target_pairs={{8,0},{16,8},{24,16},{32,24},{40,32},{48,40},{56,48},{64,56},{72,6... | collective-permute-start | bytes 24584 | tf_op jit(solution)/shard_map/ppermute | solution.py:22
  107.3 9.6 %collective-permute-start.21 = (f32[1,16,128]{2,1,0:T(8,128)S(1)}, f32[1,16,128]{2,1,0:T(8,128)S(1)}, u32[]{:S(2)}, u32[]{:S(2)}) collective-permute-start(f32[1,16,128]{2,1,0:T(8,128)S(1)} %get-tuple-element.88), channel_id=1, source_target_pairs={{0,8},{8,16},{16,24},{24,32},{32,40},{40,48},{48,56},{56,64},{64,7... | collective-permute-start | bytes 24584 | tf_op jit(solution)/shard_map/ppermute | solution.py:21
  109.8 12.4 %collective-permute-start.24 = (f32[1,8,128]{2,1,0:T(8,128)S(1)}, f32[1,8,128]{2,1,0:T(8,128)S(1)}, u32[]{:S(2)}, u32[]{:S(2)}) collective-permute-start(f32[1,8,128]{2,1,0:T(8,128)S(1)} %get-tuple-element.113), channel_id=1, source_target_pairs={{8,0},{16,8},{24,16},{32,24},{40,32},{48,40},{56,48},{64,56},{72,6... | collective-permute-start | bytes 12296 | tf_op jit(solution)/shard_map/ppermute | solution.py:22
  117.0 11.6 %collective-permute-start.22 = (f32[10,1,128]{2,1,0:T(1,128)S(1)}, f32[10,1,128]{2,1,0:T(1,128)S(1)}, u32[]{:S(2)}, u32[]{:S(2)}) collective-permute-start(f32[10,1,128]{2,1,0:T(1,128)S(1)} %get-tuple-element.78), channel_id=1, source_target_pairs={{1,0},{2,1},{3,2},{4,3},{5,4},{6,5},{7,6},{9,8},{10,9},{11,10},{12... | collective-permute-start | bytes 15368 | tf_op jit(solution)/shard_map/ppermute | solution.py:22
  120.8 7.8 %collective-permute-start.23 = (f32[10,1,128]{2,1,0:T(1,128)S(1)}, f32[10,1,128]{2,1,0:T(1,128)S(1)}, u32[]{:S(2)}, u32[]{:S(2)}) collective-permute-start(f32[10,1,128]{2,1,0:T(1,128)S(1)} %get-tuple-element.79), channel_id=1, source_target_pairs={{0,1},{1,2},{2,3},{3,4},{4,5},{5,6},{6,7},{8,9},{9,10},{10,11},{11... | collective-permute-start | bytes 15368 | tf_op jit(solution)/shard_map/ppermute | solution.py:21
  153.8 11.6 %collective-permute-start.32 = (f32[1,8,128]{2,1,0:T(8,128)S(1)}, f32[1,8,128]{2,1,0:T(8,128)S(1)}, u32[]{:S(2)}, u32[]{:S(2)}) collective-permute-start(f32[1,8,128]{2,1,0:T(8,128)S(1)} %get-tuple-element.109), channel_id=1, source_target_pairs={{8,0},{16,8},{24,16},{32,24},{40,32},{48,40},{56,48},{64,56},{72,6... | collective-permute-start | bytes 12296 | tf_op jit(solution)/shard_map/ppermute | solution.py:22
  155.7 9.6 %collective-permute-start.33 = (f32[1,8,128]{2,1,0:T(8,128)S(1)}, f32[1,8,128]{2,1,0:T(8,128)S(1)}, u32[]{:S(2)}, u32[]{:S(2)}) collective-permute-start(f32[1,8,128]{2,1,0:T(8,128)S(1)} %get-tuple-element.108), channel_id=1, source_target_pairs={{0,8},{8,16},{16,24},{24,32},{32,40},{40,48},{48,56},{56,64},{64,7... | collective-permute-start | bytes 12296 | tf_op jit(solution)/shard_map/ppermute | solution.py:21
  158.1 12.9 %collective-permute-start.36 = (f32[1,4,128]{2,1,0:T(4,128)S(1)}, f32[1,4,128]{2,1,0:T(4,128)S(1)}, u32[]{:S(2)}, u32[]{:S(2)}) collective-permute-start(f32[1,4,128]{2,1,0:T(4,128)S(1)} %get-tuple-element.135), channel_id=1, source_target_pairs={{8,0},{16,8},{24,16},{32,24},{40,32},{48,40},{56,48},{64,56},{72,6... | collective-permute-start | bytes 6152 | tf_op jit(solution)/shard_map/ppermute | solution.py:22
  163.4 7.6 %collective-permute-start.37 = (f32[1,4,128]{2,1,0:T(4,128)S(1)}, f32[1,4,128]{2,1,0:T(4,128)S(1)}, u32[]{:S(2)}, u32[]{:S(2)}) collective-permute-start(f32[1,4,128]{2,1,0:T(4,128)S(1)} %get-tuple-element.134), channel_id=1, source_target_pairs={{0,8},{8,16},{16,24},{24,32},{32,40},{40,48},{48,56},{56,64},{64,7... | collective-permute-start | bytes 6152 | tf_op jit(solution)/shard_map/ppermute | solution.py:21
  165.4 12.0 %collective-permute-start.34 = (f32[6,1,128]{2,1,0:T(1,128)S(1)}, f32[6,1,128]{2,1,0:T(1,128)S(1)}, u32[]{:S(2)}, u32[]{:S(2)}) collective-permute-start(f32[6,1,128]{2,1,0:T(1,128)S(1)} %get-tuple-element.98), channel_id=1, source_target_pairs={{1,0},{2,1},{3,2},{4,3},{5,4},{6,5},{7,6},{9,8},{10,9},{11,10},{12... | collective-permute-start | bytes 9224 | tf_op jit(solution)/shard_map/ppermute | solution.py:22
  169.7 7.6 %collective-permute-start.35 = (f32[6,1,128]{2,1,0:T(1,128)S(1)}, f32[6,1,128]{2,1,0:T(1,128)S(1)}, u32[]{:S(2)}, u32[]{:S(2)}) collective-permute-start(f32[6,1,128]{2,1,0:T(1,128)S(1)} %get-tuple-element.99), channel_id=1, source_target_pairs={{0,1},{1,2},{2,3},{3,4},{4,5},{5,6},{6,7},{8,9},{9,10},{10,11},{11... | collective-permute-start | bytes 9224 | tf_op jit(solution)/shard_map/ppermute | solution.py:21
  223.6 11.7 %collective-permute-start.49 = (f32[2,1,128]{2,1,0:T(1,128)S(1)}, f32[2,1,128]{2,1,0:T(1,128)S(1)}, u32[]{:S(2)}, u32[]{:S(2)}) collective-permute-start(f32[2,1,128]{2,1,0:T(1,128)S(1)} %get-tuple-element.154), channel_id=1, source_target_pairs={{0,1},{1,2},{2,3},{3,4},{4,5},{5,6},{6,7},{8,9},{9,10},{10,11},{11... | collective-permute-start | bytes 3080 | tf_op jit(solution)/shard_map/ppermute | solution.py:21
  224.9 10.4 %collective-permute-start.50 = (f32[2,1,128]{2,1,0:T(1,128)S(1)}, f32[2,1,128]{2,1,0:T(1,128)S(1)}, u32[]{:S(2)}, u32[]{:S(2)}) collective-permute-start(f32[2,1,128]{2,1,0:T(1,128)S(1)} %get-tuple-element.155), channel_id=1, source_target_pairs={{1,0},{2,1},{3,2},{4,3},{5,4},{6,5},{7,6},{9,8},{10,9},{11,10},{12... | collective-permute-start | bytes 3080 | tf_op jit(solution)/shard_map/ppermute | solution.py:22
  231.4 7.6 %collective-permute-start.52 = (f32[1,2,128]{2,1,0:T(2,128)S(1)}, f32[1,2,128]{2,1,0:T(2,128)S(1)}, u32[]{:S(2)}, u32[]{:S(2)}) collective-permute-start(f32[1,2,128]{2,1,0:T(2,128)S(1)} %slice_bitcast_fusion.2), channel_id=1, source_target_pairs={{0,16},{8,24},{16,32},{24,40},{32,48},{40,56},{48,64},{56,72},{64,... | collective-permute-start | bytes 3080 | tf_op jit(solution)/shard_map/ppermute | solution.py:30
  239.1 11.7 %collective-permute-start.53 = (f32[2,1,128]{2,1,0:T(1,128)S(1)}, f32[2,1,128]{2,1,0:T(1,128)S(1)}, u32[]{:S(2)}, u32[]{:S(2)}) collective-permute-start(f32[2,1,128]{2,1,0:T(1,128)S(1)} %get-tuple-element.153), channel_id=1, source_target_pairs={{0,1},{1,2},{2,3},{3,4},{4,5},{5,6},{6,7},{8,9},{9,10},{10,11},{11... | collective-permute-start | bytes 3080 | tf_op jit(solution)/shard_map/ppermute | solution.py:21
  240.4 10.4 %collective-permute-start.54 = (f32[2,1,128]{2,1,0:T(1,128)S(1)}, f32[2,1,128]{2,1,0:T(1,128)S(1)}, u32[]{:S(2)}, u32[]{:S(2)}) collective-permute-start(f32[2,1,128]{2,1,0:T(1,128)S(1)} %get-tuple-element.152), channel_id=1, source_target_pairs={{1,0},{2,1},{3,2},{4,3},{5,4},{6,5},{7,6},{9,8},{10,9},{11,10},{12... | collective-permute-start | bytes 3080 | tf_op jit(solution)/shard_map/ppermute | solution.py:22
  246.9 7.6 %collective-permute-start.56 = (f32[1,2,128]{2,1,0:T(2,128)S(1)}, f32[1,2,128]{2,1,0:T(2,128)S(1)}, u32[]{:S(2)}, u32[]{:S(2)}) collective-permute-start(f32[1,2,128]{2,1,0:T(2,128)S(1)} %get-tuple-element.151), channel_id=1, source_target_pairs={{0,16},{8,24},{16,32},{24,40},{32,48},{40,56},{48,64},{56,72},{64,... | collective-permute-start | bytes 3080 | tf_op jit(solution)/shard_map/ppermute | solution.py:30
  254.6 11.7 %collective-permute-start.57 = (f32[2,1,128]{2,1,0:T(1,128)S(1)}, f32[2,1,128]{2,1,0:T(1,128)S(1)}, u32[]{:S(2)}, u32[]{:S(2)}) collective-permute-start(f32[2,1,128]{2,1,0:T(1,128)S(1)} %get-tuple-element.149), channel_id=1, source_target_pairs={{0,1},{1,2},{2,3},{3,4},{4,5},{5,6},{6,7},{8,9},{9,10},{10,11},{11... | collective-permute-start | bytes 3080 | tf_op jit(solution)/shard_map/ppermute | solution.py:21
  255.9 10.4 %collective-permute-start.58 = (f32[2,1,128]{2,1,0:T(1,128)S(1)}, f32[2,1,128]{2,1,0:T(1,128)S(1)}, u32[]{:S(2)}, u32[]{:S(2)}) collective-permute-start(f32[2,1,128]{2,1,0:T(1,128)S(1)} %get-tuple-element.148), channel_id=1, source_target_pairs={{1,0},{2,1},{3,2},{4,3},{5,4},{6,5},{7,6},{9,8},{10,9},{11,10},{12... | collective-permute-start | bytes 3080 | tf_op jit(solution)/shard_map/ppermute | solution.py:22
  262.4 7.6 %collective-permute-start.60 = (f32[1,2,128]{2,1,0:T(2,128)S(1)}, f32[1,2,128]{2,1,0:T(2,128)S(1)}, u32[]{:S(2)}, u32[]{:S(2)}) collective-permute-start(f32[1,2,128]{2,1,0:T(2,128)S(1)} %get-tuple-element.147), channel_id=1, source_target_pairs={{0,16},{8,24},{16,32},{24,40},{32,48},{40,56},{48,64},{56,72},{64,... | collective-permute-start | bytes 3080 | tf_op jit(solution)/shard_map/ppermute | solution.py:30
  275.6 16.3 %collective-permute-start.62 = (f32[2,1,128]{2,0,1:T(2,128)S(1)}, f32[2,1,128]{2,0,1:T(2,128)S(1)}, u32[]{:S(2)}, u32[]{:S(2)}) collective-permute-start(f32[2,1,128]{2,0,1:T(2,128)S(1)} %slice_bitcast_fusion), channel_id=1, source_target_pairs={{0,1},{1,2},{2,3},{3,4},{4,5},{5,6},{6,7},{8,9},{9,10},{10,11},{11... | collective-permute-start | bytes 3080 | tf_op jit(solution)/shard_map/ppermute | solution.py:21
  276.9 15.0 %collective-permute-start.63 = (f32[2,1,128]{2,0,1:T(2,128)S(1)}, f32[2,1,128]{2,0,1:T(2,128)S(1)}, u32[]{:S(2)}, u32[]{:S(2)}) collective-permute-start(f32[2,1,128]{2,0,1:T(2,128)S(1)} %slice_bitcast_fusion), channel_id=1, source_target_pairs={{1,0},{2,1},{3,2},{4,3},{5,4},{6,5},{7,6},{9,8},{10,9},{11,10},{12... | collective-permute-start | bytes 3080 | tf_op jit(solution)/shard_map/ppermute | solution.py:22
  283.4 8.4 %collective-permute-start.65 = (f32[1,1,128]{2,0,1:T(1,128)S(1)}, f32[1,1,128]{2,0,1:T(1,128)S(1)}, u32[]{:S(2)}, u32[]{:S(2)}) collective-permute-start(f32[1,1,128]{2,0,1:T(1,128)S(1)} %slice_bitcast_fusion.4), channel_id=1, source_target_pairs={{0,32},{8,40},{16,48},{24,56},{32,64},{40,72},{48,80},{56,88},{64,... | collective-permute-start | bytes 1544 | tf_op jit(solution)/shard_map/ppermute | solution.py:30
  291.9 17.3 %collective-permute-start.66 = (f32[2,1,128]{2,0,1:T(2,128)S(1)}, f32[2,1,128]{2,0,1:T(2,128)S(1)}, u32[]{:S(2)}, u32[]{:S(2)}) collective-permute-start(f32[2,1,128]{2,0,1:T(2,128)S(1)} %get-tuple-element.13), channel_id=1, source_target_pairs={{0,1},{1,2},{2,3},{3,4},{4,5},{5,6},{6,7},{8,9},{9,10},{10,11},{11... | collective-permute-start | bytes 3080 | tf_op jit(solution)/shard_map/ppermute | solution.py:21
  293.2 16.0 %collective-permute-start.67 = (f32[2,1,128]{2,0,1:T(2,128)S(1)}, f32[2,1,128]{2,0,1:T(2,128)S(1)}, u32[]{:S(2)}, u32[]{:S(2)}) collective-permute-start(f32[2,1,128]{2,0,1:T(2,128)S(1)} %get-tuple-element.13), channel_id=1, source_target_pairs={{1,0},{2,1},{3,2},{4,3},{5,4},{6,5},{7,6},{9,8},{10,9},{11,10},{12... | collective-permute-start | bytes 3080 | tf_op jit(solution)/shard_map/ppermute | solution.py:22
  300.8 8.4 %collective-permute-start.69 = (f32[1,1,128]{2,0,1:T(1,128)S(1)}, f32[1,1,128]{2,0,1:T(1,128)S(1)}, u32[]{:S(2)}, u32[]{:S(2)}) collective-permute-start(f32[1,1,128]{2,0,1:T(1,128)S(1)} %get-tuple-element.161), channel_id=1, source_target_pairs={{0,32},{8,40},{16,48},{24,56},{32,64},{40,72},{48,80},{56,88},{64,... | collective-permute-start | bytes 1544 | tf_op jit(solution)/shard_map/ppermute | solution.py:30
  309.3 17.9 %collective-permute-start.70 = (f32[2,1,128]{2,0,1:T(2,128)S(1)}, f32[2,1,128]{2,0,1:T(2,128)S(1)}, u32[]{:S(2)}, u32[]{:S(2)}) collective-permute-start(f32[2,1,128]{2,0,1:T(2,128)S(1)} %divide_add_fusion.4), channel_id=1, source_target_pairs={{0,1},{1,2},{2,3},{3,4},{4,5},{5,6},{6,7},{8,9},{9,10},{10,11},{11... | collective-permute-start | bytes 3080 | tf_op jit(solution)/shard_map/ppermute | solution.py:21
  310.6 16.6 %collective-permute-start.71 = (f32[2,1,128]{2,0,1:T(2,128)S(1)}, f32[2,1,128]{2,0,1:T(2,128)S(1)}, u32[]{:S(2)}, u32[]{:S(2)}) collective-permute-start(f32[2,1,128]{2,0,1:T(2,128)S(1)} %divide_add_fusion.4), channel_id=1, source_target_pairs={{1,0},{2,1},{3,2},{4,3},{5,4},{6,5},{7,6},{9,8},{10,9},{11,10},{12... | collective-permute-start | bytes 3080 | tf_op jit(solution)/shard_map/ppermute | solution.py:22
  318.7 8.4 %collective-permute-start.73 = (f32[1,1,128]{2,0,1:T(1,128)S(1)}, f32[1,1,128]{2,0,1:T(1,128)S(1)}, u32[]{:S(2)}, u32[]{:S(2)}) collective-permute-start(f32[1,1,128]{2,0,1:T(1,128)S(1)} %get-tuple-element.159), channel_id=1, source_target_pairs={{0,32},{8,40},{16,48},{24,56},{32,64},{40,72},{48,80},{56,88},{64,... | collective-permute-start | bytes 1544 | tf_op jit(solution)/shard_map/ppermute | solution.py:30
  327.3 18.9 %collective-permute-start.74 = (f32[2,1,128]{2,0,1:T(2,128)S(1)}, f32[2,1,128]{2,0,1:T(2,128)S(1)}, u32[]{:S(2)}, u32[]{:S(2)}) collective-permute-start(f32[2,1,128]{2,0,1:T(2,128)S(1)} %divide_add_fusion.3), channel_id=1, source_target_pairs={{0,1},{1,2},{2,3},{3,4},{4,5},{5,6},{6,7},{8,9},{9,10},{10,11},{11... | collective-permute-start | bytes 3080 | tf_op jit(solution)/shard_map/ppermute | solution.py:21
  328.6 17.6 %collective-permute-start.75 = (f32[2,1,128]{2,0,1:T(2,128)S(1)}, f32[2,1,128]{2,0,1:T(2,128)S(1)}, u32[]{:S(2)}, u32[]{:S(2)}) collective-permute-start(f32[2,1,128]{2,0,1:T(2,128)S(1)} %divide_add_fusion.3), channel_id=1, source_target_pairs={{1,0},{2,1},{3,2},{4,3},{5,4},{6,5},{7,6},{9,8},{10,9},{11,10},{12... | collective-permute-start | bytes 3080 | tf_op jit(solution)/shard_map/ppermute | solution.py:22
  337.7 8.4 %collective-permute-start.77 = (f32[1,1,128]{2,0,1:T(1,128)S(1)}, f32[1,1,128]{2,0,1:T(1,128)S(1)}, u32[]{:S(2)}, u32[]{:S(2)}) collective-permute-start(f32[1,1,128]{2,0,1:T(1,128)S(1)} %get-tuple-element.157), channel_id=1, source_target_pairs={{0,32},{8,40},{16,48},{24,56},{32,64},{40,72},{48,80},{56,88},{64,... | collective-permute-start | bytes 1544 | tf_op jit(solution)/shard_map/ppermute | solution.py:30
  346.3 12.9 %collective-permute-start.78 = (f32[2,1,128]{2,1,0:T(1,128)S(1)}, f32[2,1,128]{2,1,0:T(1,128)S(1)}, u32[]{:S(2)}, u32[]{:S(2)}) collective-permute-start(f32[2,1,128]{2,1,0:T(1,128)S(1)} %get-tuple-element.145), channel_id=1, source_target_pairs={{0,1},{1,2},{2,3},{3,4},{4,5},{5,6},{6,7},{8,9},{9,10},{10,11},{11... | collective-permute-start | bytes 3080 | tf_op jit(solution)/shard_map/ppermute | solution.py:21
  347.6 11.6 %collective-permute-start.79 = (f32[2,1,128]{2,1,0:T(1,128)S(1)}, f32[2,1,128]{2,1,0:T(1,128)S(1)}, u32[]{:S(2)}, u32[]{:S(2)}) collective-permute-start(f32[2,1,128]{2,1,0:T(1,128)S(1)} %get-tuple-element.144), channel_id=1, source_target_pairs={{1,0},{2,1},{3,2},{4,3},{5,4},{6,5},{7,6},{9,8},{10,9},{11,10},{12... | collective-permute-start | bytes 3080 | tf_op jit(solution)/shard_map/ppermute | solution.py:22
  355.3 7.6 %collective-permute-start.81 = (f32[1,2,128]{2,1,0:T(2,128)S(1)}, f32[1,2,128]{2,1,0:T(2,128)S(1)}, u32[]{:S(2)}, u32[]{:S(2)}) collective-permute-start(f32[1,2,128]{2,1,0:T(2,128)S(1)} %get-tuple-element.143), channel_id=1, source_target_pairs={{0,16},{8,24},{16,32},{24,40},{32,48},{40,56},{48,64},{56,72},{64,... | collective-permute-start | bytes 3080 | tf_op jit(solution)/shard_map/ppermute | solution.py:30
  363.0 13.0 %collective-permute-start.82 = (f32[2,1,128]{2,1,0:T(1,128)S(1)}, f32[2,1,128]{2,1,0:T(1,128)S(1)}, u32[]{:S(2)}, u32[]{:S(2)}) collective-permute-start(f32[2,1,128]{2,1,0:T(1,128)S(1)} %get-tuple-element.141), channel_id=1, source_target_pairs={{0,1},{1,2},{2,3},{3,4},{4,5},{5,6},{6,7},{8,9},{9,10},{10,11},{11... | collective-permute-start | bytes 3080 | tf_op jit(solution)/shard_map/ppermute | solution.py:21
  364.3 11.7 %collective-permute-start.83 = (f32[2,1,128]{2,1,0:T(1,128)S(1)}, f32[2,1,128]{2,1,0:T(1,128)S(1)}, u32[]{:S(2)}, u32[]{:S(2)}) collective-permute-start(f32[2,1,128]{2,1,0:T(1,128)S(1)} %get-tuple-element.140), channel_id=1, source_target_pairs={{1,0},{2,1},{3,2},{4,3},{5,4},{6,5},{7,6},{9,8},{10,9},{11,10},{12... | collective-permute-start | bytes 3080 | tf_op jit(solution)/shard_map/ppermute | solution.py:22
  372.0 7.6 %collective-permute-start.85 = (f32[1,2,128]{2,1,0:T(2,128)S(1)}, f32[1,2,128]{2,1,0:T(2,128)S(1)}, u32[]{:S(2)}, u32[]{:S(2)}) collective-permute-start(f32[1,2,128]{2,1,0:T(2,128)S(1)} %get-tuple-element.139), channel_id=1, source_target_pairs={{0,16},{8,24},{16,32},{24,40},{32,48},{40,56},{48,64},{56,72},{64,... | collective-permute-start | bytes 3080 | tf_op jit(solution)/shard_map/ppermute | solution.py:30
  494.1 7.2 %collective-permute-start.111 = (f32[1,32,128]{2,1,0:T(8,128)S(1)}, f32[1,32,128]{2,1,0:T(8,128)S(1)}, u32[]{:S(2)}, u32[]{:S(2)}) collective-permute-start(f32[1,32,128]{2,1,0:T(8,128)S(1)} %get-tuple-element.66), channel_id=1, source_target_pairs={{0,8},{8,16},{16,24},{24,32},{32,40},{40,48},{48,56},{56,64},{64,7... | collective-permute-start | bytes 49160 | tf_op jit(solution)/shard_map/ppermute | solution.py:21
  (72 other events, 421.6 us)
where the time goes:
time: 533 us; the launch traced here: 529 us
  starting transfers between devices  329 us (62%)
  waiting for transfers between devices  173 us (32%)
  other arithmetic  17 us (3%)
  local copies, waits for them, and re-layouts  8.47 us (2%)
    ppermute x49, starting transfers between devices, extended(): after = lax.ppermute(initial, axis, down)  187 us
    ppermute x49, waiting for transfers between devices, extended(): before = lax.ppermute(last, axis, up)  134 us
    ppermute x49, starting transfers between devices, extended(): before = lax.ppermute(last, axis, up)  82.3 us
    ppermute x18, starting transfers between devices, shifted(): lax.ppermute(value, axis, [(source, source + steps) for source in range(i...  56.2 us
    ppermute x18, waiting for transfers between devices, shifted(): lax.ppermute(value, axis, [(source, source + steps) for source in range(i...  34.2 us
  transfers between devices with their start and end apart: 118, of which 45 were waited for; matrix products, arithmetic and copies ran while one was open for 1% of the time, Pallas kernels for 0%

commit v1 on v0

v1 whole, which is shorter than its diff:
```python
import functools

import jax
import jax.numpy as jnp
from jax import lax
from jax.experimental import pallas as pl
from jax.experimental.pallas import tpu as pltpu
from jax.sharding import PartitionSpec as P

MESH = pl.DeviceIdType.MESH
F32 = jnp.float32
LEVELS = 6
TYPES = 8
HZ = 0.5 * 0.015625
REACH = (3, 4, 5, 5, 5, 5)


class Level:
    def __init__(self, index, rows, columns, across, blk):
        self.index, self.rows, self.columns, self.across, self.blk = index, rows, columns, across, blk
        self.reach = REACH[index]
        self.ox = self.reach + 1
        self.nx = rows + 2 * self.ox + 2
        if across:
            self.cy = columns
            self.oy = 8
            self.ny = 8 + columns + 8
        else:
            self.cy = -(-(columns + 2 * self.reach) // 8) * 8
            self.oy = 8 + (self.cy - columns) // 2
            self.ny = self.cy + 16
        self.y = pl.ds(8, self.cy)
        self.own_x = pl.ds(self.ox, rows)
        self.own_y = pl.ds(self.oy, columns)
        self.half = 0.5 * 0.25**index

    def shape(self, *lead):
        return (*lead, self.nx, self.ny, 128)

    def span(self, radius):
        first = self.ox - radius
        count = self.rows + 2 * radius
        return first, -(-count // self.blk) * self.blk // self.blk


def overlap(size, step, radius):
    low = max(-radius, -step * size)
    high = min(size + radius, (1 - step) * size)
    return low + step * size, low, high - low


def kernel(sizes, levels, src_ref, tis_ref, dif_ref, upt_ref, out_ref, *scratch):
    gx_count, gy_count = sizes
    names = iter(scratch)
    tis = next(names)
    coef = [next(names) for _ in levels]
    right = [next(names) for _ in levels]
    kap = [next(names) for _ in levels]
    wgt = [next(names) for _ in levels]
    inv = [next(names) for _ in levels]
    dia = [next(names) for _ in levels]
    one = [next(names) for _ in levels]
    two = [next(names) for _ in levels]
    tri = [next(names) for _ in levels]
    gat_c, gat_b = next(names), next(names)
    local_sem, send_sem, recv_sem = next(names), next(names), next(names)

    gx = lax.axis_index("gx")
    gy = lax.axis_index("gy")
    parity = lax.rem(gx, 2)
    places = {}

    def device(dx, dy):
        if ("x", dx) not in places:
            places["x", dx] = lax.rem(gx + (dx + gx_count), gx_count) if dx else gx
        if ("y", dy) not in places:
            places["y", dy] = lax.rem(gy + (dy + gy_count), gy_count) if dy else gy
        return places["x", dx], places["y", dy]

    counter = [0]

    def remote(source, target, dx, dy):
        number = counter[0]
        counter[0] += 1
        copy = pltpu.make_async_remote_copy(
            src_ref=source,
            dst_ref=target,
            send_sem=send_sem.at[number],
            recv_sem=recv_sem.at[number],
            device_id=device(dx, dy),
            device_id_type=MESH,
        )
        copy.start()
        return copy

    def arrived(copies):
        for copy in copies:
            copy.wait_recv()

    def left(copies):
        for copy in copies:
            copy.wait_send()

    def around(level, radius):
        far = -(-radius // level.rows)
        return [(dx, dy) for dx in range(-far, far + 1) for dy in (-1, 0, 1) if (dx, dy) != (0, 0)]

    def send_block(ref, level, radius, lead=()):
        copies = []
        for dx, dy in around(level, radius):
            sx, tx, cx = overlap(level.rows, dx, radius)
            sy, ty, cy = overlap(level.columns, dy, radius)
            source = ref.at[(*lead, pl.ds(level.ox + sx, cx), pl.ds(level.oy + sy, cy))]
            target = ref.at[(*lead, pl.ds(level.ox + tx, cx), pl.ds(level.oy + ty, cy))]
            copies.append(remote(source, target, dx, dy))
        return copies

    def send_rows(ref, level, radius, lead=(), stride=1):
        copies = []
        far = -(-radius // level.rows)
        for step in range(1, far + 1):
            for dx in (step, -step):
                sx, tx, cx = overlap(level.rows, dx, radius)
                source = ref.at[(*lead, pl.ds(level.ox + sx, cx), level.y)]
                target = ref.at[(*lead, pl.ds(level.ox + tx, cx), level.y)]
                copies.append(remote(source, target, dx * stride, 0))
        return copies

    def send_columns(ref):
        return [remote(ref.at[gy], ref.at[gy], 0, dy) for dy in range(1, gy_count)]

    def loop(count, step):
        def body(i, carry):
            step(i)
            return carry

        lax.fori_loop(0, count, body, 0)

    def inside(level, x, blk, y, cy):
        base = gx // 2 if level.index == LEVELS - 1 else gx
        total = level.rows * (gx_count // 2 if level.index == LEVELS - 1 else gx_count)
        row = lax.broadcasted_iota(jnp.int32, (blk, cy, 128), 0) + (base * level.rows + x - level.ox)
        good = (row >= 0) & (row < total)
        if not level.across:
            column = lax.broadcasted_iota(jnp.int32, (blk, cy, 128), 1) + (gy * level.columns + y - level.oy)
            good = good & (column >= 0) & (column < level.columns * gy_count)
        return good

    def types(x, blk, y, cy, masked):
        zero = levels[0]
        kind = tis[pl.ds(x, blk), pl.ds(y, cy), :]
        kappa = jnp.full(kind.shape, dif_ref[0], F32)
        sigma = jnp.full(kind.shape, upt_ref[0], F32)
        for index in range(1, TYPES):
            hit = kind == index
            kappa = jnp.where(hit, dif_ref[index], kappa)
            sigma = jnp.where(hit, upt_ref[index], sigma)
        if masked:
            kappa = jnp.where(inside(zero, x, blk, y, cy), kappa, 0.0)
        kap[0][pl.ds(x, blk), pl.ds(y, cy), :] = kappa
        coef[0][pl.ds(x, blk), pl.ds(y, cy), :] = sigma

    def mean(ref, lead, x, y, count):
        even = pl.ds(y, count, stride=2)
        odd = pl.ds(y + 1, count, stride=2)
        near = ref[(*lead, x, even, slice(None))] + ref[(*lead, x + 1, even, slice(None))]
        far = ref[(*lead, x, odd, slice(None))] + ref[(*lead, x + 1, odd, slice(None))]
        return 0.25 * (near + far)

    def masked_kappa(level):
        index = level.index
        first, count = level.span(level.reach + 1)
        y, cy = (8, level.cy) if level.across else (7, level.cy + 2)

        def step(i):
            x = first + i * level.blk
            value = coef[index][0, pl.ds(x, level.blk), pl.ds(y, cy), :]
            value = jnp.where(inside(level, x, level.blk, y, cy), value, 0.0)
            kap[index][pl.ds(x, level.blk), pl.ds(y, cy), :] = value

        loop(count, step)

    def weights(level):
        index, blk, cy = level.index, level.blk, level.cy
        first, count = level.span(level.reach)
        field = kap[index]
        half = level.half

        def step(i):
            x = first + i * blk
            here = (pl.ds(x, blk), level.y, slice(None))
            centre = field[here]
            sigma = coef[index][here] if index == 0 else coef[index][(1, *here)]
            plane = lax.broadcasted_iota(jnp.int32, centre.shape, 2)
            top, bottom = plane == 127, plane == 0
            east = half * (centre + field[pl.ds(x + 1, blk), level.y, :])
            west = half * (centre + field[pl.ds(x - 1, blk), level.y, :])
            north = half * (centre + field[pl.ds(x, blk), pl.ds(9, cy), :])
            south = half * (centre + field[pl.ds(x, blk), pl.ds(7, cy), :])
            upper = HZ * (centre + jnp.where(top, 0.0, pltpu.roll(centre, 127, 2)))
            lower = HZ * (centre + jnp.where(bottom, 0.0, pltpu.roll(centre, 1, 2)))
            diag = east + west + north + south + upper + lower + sigma
            inverse = jnp.where(inside(level, x, blk, 8, cy), 0.8 / diag, 0.0)
            inv[index][here] = inverse
            dia[index][here] = 1.25 * diag
            out = wgt[index]
            out[(0, *here)] = inverse * east
            out[(1, *here)] = inverse * west
            out[(2, *here)] = inverse * north
            out[(3, *here)] = inverse * south
            out[(4, *here)] = jnp.where(top, 0.0, inverse * upper)
            out[(5, *here)] = jnp.where(bottom, 0.0, inverse * lower)

        loop(count, step)

    def pulled(level, field, x, blk, centre):
        index, cy = level.index, level.cy
        here = (pl.ds(x, blk), level.y, slice(None))
        weight = wgt[index]
        total = one[index][here] + weight[(0, *here)] * field[pl.ds(x + 1, blk), level.y, :]
        other = weight[(1, *here)] * field[pl.ds(x - 1, blk), level.y, :]
        total = total + weight[(2, *here)] * field[pl.ds(x, blk), pl.ds(9, cy), :]
        other = other + weight[(3, *here)] * field[pl.ds(x, blk), pl.ds(7, cy), :]
        total = total + weight[(4, *here)] * pltpu.roll(centre, 127, 2)
        other = other + weight[(5, *here)] * pltpu.roll(centre, 1, 2)
        return total + other

    def first_sweep(level):
        index, blk = level.index, level.blk
        first, count = level.span(level.reach)

        def step(i):
            here = (pl.ds(first + i * blk, blk), level.y, slice(None))
            one[index][here] = inv[index][here] * right[index][here]

        loop(count, step)

    def sweep(level, source, target, radius):
        blk = level.blk
        first, count = level.span(radius)

        def step(i):
            x = first + i * blk
            here = (pl.ds(x, blk), level.y, slice(None))
            centre = source[here]
            target[here] = 0.2 * centre + pulled(level, source, x, blk, centre)

        loop(count, step)

    def residual(level, radius):
        index, blk = level.index, level.blk
        first, count = level.span(radius)

        def step(i):
            x = first + i * blk
            here = (pl.ds(x, blk), level.y, slice(None))
            centre = two[index][here]
            total = pulled(level, two[index], x, blk, centre)
            tri[index][here] = dia[index][here] * (total - 0.8 * centre)

        loop(count, step)

    def lift(value, level, x, y, count):
        for row in (x, x + 1):
            for column in (y, y + 1):
                spot = (row, pl.ds(column, count, stride=2), slice(None))
                two[level.index][spot] = two[level.index][spot] + value

    zero, one_, two_, three, four, five = levels

    loads = []
    for position, (source, target) in enumerate(((tis_ref, tis), (src_ref, right[0]))):
        copy = pltpu.make_async_copy(source, target.at[zero.own_x, zero.own_y], local_sem.at[position])
        copy.start()
        loads.append(copy)
    barrier = pltpu.get_barrier_semaphore()
    greeted = around(two_, two_.reach + 1)
    greeted = greeted + [(0, dy) for dy in range(2, gy_count - 1)]
    for dx, dy in greeted:
        pl.semaphore_signal(barrier, inc=1, device_id=device(dx, dy), device_id_type=MESH)
    for level in (three, four, five):
        index = level.index
        for ref in (kap[index], one[index], two[index], tri[index]):
            ref[:, pl.ds(0, 8), :] = jnp.zeros((level.nx, 8, 128), F32)
            ref[:, pl.ds(8 + level.cy, 8), :] = jnp.zeros((level.nx, 8, 128), F32)
    loads[0].wait()
    loads[1].wait()
    pl.semaphore_wait(barrier, len(greeted))

    sent_tis = send_block(tis, zero, zero.reach + 1)
    sent_src = send_block(right[0], zero, zero.reach)
    loop(zero.rows // 2, lambda i: types(zero.ox + 2 * i, 2, zero.oy, zero.columns, False))

    def coarsen(ref, lead, fine, level, field):
        def step(i):
            value = mean(ref, lead, fine.ox + 2 * i, fine.oy, level.columns)
            coef[level.index][field, level.ox + i, level.own_y, :] = value

        loop(level.rows, step)

    coarsen(kap[0], (), zero, one_, 0)
    coarsen(coef[0], (), zero, one_, 1)
    sent_c1 = send_block(coef[1], one_, one_.reach + 1, (slice(None),))
    for field in (0, 1):
        coarsen(coef[1], (field,), one_, two_, field)
    sent_c2 = send_block(coef[2], two_, two_.reach + 1, (slice(None),))
    for field in (0, 1):
        for row in (0, 1):
            gat_c[gy, field, row] = mean(coef[2], (field,), two_.ox + 2 * row, two_.oy, 4)
    sent_c3 = send_columns(gat_c)

    arrived(sent_tis)
    ring = zero.reach + 1
    edges = ring // 2
    loop(edges, lambda i: types(zero.ox - ring + 2 * i, 2, 8, zero.cy, True))
    loop(edges, lambda i: types(zero.ox + zero.rows + 2 * i, 2, 8, zero.cy, True))
    loop(zero.rows // 4, lambda i: types(zero.ox + 4 * i, 4, 8, ring, True))
    loop(zero.rows // 4, lambda i: types(zero.ox + 4 * i, 4, zero.oy + zero.columns, ring, True))
    weights(zero)
    arrived(sent_src)

    def descend(level):
        index = level.index
        first_sweep(level)
        sweep(level, one[index], two[index], level.reach - 1)
        residual(level, 0)

    def restrict_to(fine, level):
        def step(i):
            value = mean(tri[fine.index], (), fine.ox + 2 * i, fine.oy, level.columns)
            right[level.index][level.ox + i, level.own_y, :] = value

        loop(level.rows, step)

    descend(zero)
    restrict_to(zero, one_)
    sent_b1 = send_block(right[1], one_, one_.reach)
    left(sent_tis)
    left(sent_src)
    arrived(sent_c1)
    masked_kappa(one_)
    weights(one_)

    arrived(sent_b1)
    descend(one_)
    restrict_to(one_, two_)
    sent_b2 = send_block(right[2], two_, two_.reach)
    arrived(sent_c2)
    masked_kappa(two_)
    weights(two_)
    arrived(sent_c3)

    def unpack(read, write):
        for part in range(gy_count):
            for row in (0, 1):
                write(row, pl.ds(8 + 4 * part, 4), read(part, row))

    for field in (0, 1):

        def write(row, columns, value):
            coef[3][field, three.ox + row, columns, :] = value

        unpack(lambda part, row: gat_c[part, field, row], write)
    sent_x3 = send_rows(coef[3], three, three.reach + 1, (slice(None),))
    for field in (0, 1):
        coef[4][field, four.ox, four.y, :] = mean(coef[3], (field,), three.ox, 8, four.cy)
    left(sent_c1)
    left(sent_c2)
    left(sent_c3)
    left(sent_b1)

    arrived(sent_b2)
    descend(two_)
    for row in (0, 1):
        gat_b[gy, row] = mean(tri[2], (), two_.ox + 2 * row, two_.oy, 4)
    sent_b3 = send_columns(gat_b)
    sent_c4 = send_rows(coef[4], four, four.reach + 1, (slice(None),))
    arrived(sent_x3)
    masked_kappa(three)
    weights(three)
    left(sent_b2)

    arrived(sent_b3)

    def write_right(row, columns, value):
        right[3][three.ox + row, columns, :] = value

    unpack(lambda part, row: gat_b[part, row], write_right)
    sent_r3 = send_rows(right[3], three, three.reach)
    arrived(sent_c4)
    chip = four.ox - parity
    for field in (0, 1):
        coef[5][field, five.ox, five.y, :] = mean(coef[4], (field,), chip, 8, five.cy)
    sent_c5 = send_rows(coef[5], five, five.reach + 1, (slice(None),), 2)
    masked_kappa(four)
    weights(four)
    left(sent_x3)
    left(sent_b3)
    left(sent_c4)
    arrived(sent_r3)
    descend(three)
    right[4][four.ox, four.y, :] = mean(tri[3], (), three.ox, 8, four.cy)

    sent_r4 = send_rows(right[4], four, four.reach)
    arrived(sent_c5)
    masked_kappa(five)
    weights(five)
    left(sent_r3)
    left(sent_c5)
    arrived(sent_r4)
    first_sweep(four)
    sweep(four, one[4], two[4], four.reach - 1)
    residual(four, 1)
    right[5][five.ox, five.y, :] = mean(tri[4], (), chip, 8, five.cy)

    sent_r5 = send_rows(right[5], five, five.reach, (), 2)
    left(sent_r4)
    arrived(sent_r5)
    first_sweep(five)
    sweep(five, one[5], two[5], 4)
    sweep(five, two[5], tri[5], 3)
    sweep(five, tri[5], two[5], 2)
    left(sent_r5)

    def ascend(level, last):
        index = level.index
        sweep(level, two[index], tri[index], last + 1)
        sweep(level, tri[index], two[index], last)

    for offset in range(-4, 5):
        row = five.ox - 4 + (parity + (offset + 8)) // 2
        value = two[5][row, five.y, :]
        for column in (8, 9):
            spot = (four.ox + offset, pl.ds(column, five.cy, stride=2), slice(None))
            two[4][spot] = two[4][spot] + value
    ascend(four, 2)
    for offset in range(-2, 3):
        lift(two[4][four.ox + offset, four.y, :], three, three.ox + 2 * offset, 8, four.cy)
    ascend(three, 2)
    for offset in range(-2, 4):
        value = two[3][three.ox + offset, pl.ds(6 + 4 * gy, 8), :]
        lift(value, two_, two_.ox + 2 * offset, two_.oy - 4, 8)
    ascend(two_, 2)

    def lift_one(i):
        value = two[2][two_.ox - 2 + i, pl.ds(two_.oy - 2, two_.columns + 4), :]
        lift(value, one_, one_.ox - 4 + 2 * i, one_.oy - 4, two_.columns + 4)

    loop(two_.rows + 4, lift_one)
    ascend(one_, 1)

    def lift_zero(i):
        value = two[1][one_.ox - 1 + i, pl.ds(one_.oy - 1, one_.columns + 2), :]
        lift(value, zero, zero.ox - 2 + 2 * i, zero.oy - 2, one_.columns + 2)

    loop(one_.rows + 2, lift_zero)
    ascend(zero, 0)

    def store(i):
        out_ref[pl.ds(2 * i, 2)] = two[0][pl.ds(zero.ox + 2 * i, 2), zero.own_y, :]

    loop(zero.rows // 2, store)


def build(mesh, rows, columns):
    gx_count, gy_count = mesh.shape["gx"], mesh.shape["gy"]
    levels = [
        Level(0, rows, columns, False, 2),
        Level(1, rows // 2, columns // 2, False, 2),
        Level(2, rows // 4, columns // 4, False, 2),
        Level(3, rows // 8, columns // 8 * gy_count, True, 2),
        Level(4, rows // 16, columns // 16 * gy_count, True, 3),
        Level(5, 1, columns // 32 * gy_count, True, 3),
    ]
    zero = levels[0]
    messages = 160
    scratch = [pltpu.VMEM(zero.shape(), jnp.int32)]
    scratch += [pltpu.VMEM(level.shape(2) if level.index else level.shape(), F32) for level in levels]
    scratch += [pltpu.VMEM(level.shape(), F32) for level in levels]
    scratch += [pltpu.VMEM(level.shape(), F32) for level in levels]
    scratch += [pltpu.VMEM(level.shape(6), F32) for level in levels]
    for _ in range(5):
        scratch += [pltpu.VMEM(level.shape(), F32) for level in levels]
    scratch += [
        pltpu.VMEM((gy_count, 2, 2, 4, 128), F32),
        pltpu.VMEM((gy_count, 2, 4, 128), F32),
        pltpu.SemaphoreType.DMA((2,)),
        pltpu.SemaphoreType.DMA((messages,)),
        pltpu.SemaphoreType.DMA((messages,)),
    ]
    return pl.pallas_call(
        functools.partial(kernel, (gx_count, gy_count), levels),
        out_shape=jax.ShapeDtypeStruct((rows, columns, 128), F32),
        in_specs=[
            pl.BlockSpec(memory_space=pl.ANY),
            pl.BlockSpec(memory_space=pl.ANY),
            pl.BlockSpec(memory_space=pltpu.SMEM),
            pl.BlockSpec(memory_space=pltpu.SMEM),
        ],
        out_specs=pl.BlockSpec(memory_space=pltpu.VMEM),
        scratch_shapes=scratch,
        name="vcycle",
        compiler_params=pltpu.CompilerParams(
            collective_id=0, has_side_effects=True, vmem_limit_bytes=40 * 2**20
        ),
    )


def solution(mesh):
    def body(source, tissue, diffusivity, uptake):
        call = build(mesh, source.shape[0], source.shape[1])
        return call(source, tissue, diffusivity, uptake)

    in_specs = (P("gx", "gy", None), P("gx", "gy", None), P(), P())
    out_specs = P("gx", "gy", None)
    return jax.shard_map(body, mesh=mesh, in_specs=in_specs, out_specs=out_specs, check_vma=False)
```

time: 533 us -> 72.1 us (0.14)
  the two profiles are of different devices: /device:TPU:62 before, /device:TPU:1 now
where the time goes in v1:
time: 72.1 us; the launch traced here: 71.9 us
  Pallas kernels  68 us (94%)
  local copies, waits for them, and re-layouts  3.91 us (5%)
    pallas_call x1, Pallas kernels, body(): return call(source, tissue, diffusivity, uptake)  68 us
    unnamed x9, local copies, waits for them, and re-layouts  3.91 us

profile of v1, /device:TPU:1, one launch (start us, length us, event | category | flops | bytes accessed | tf_op | source)
XLA Modules:
  0.0 71.9 jit_solution(700612964359878033)
XLA Ops:
  0.0 0.0 copy-start
  0.0 0.9 %copy-done = f32[16,32,128]{2,1,0:T(8,128)S(1)} copy-done((f32[16,32,128]{2,1,0:T(8,128)S(1)}, f32[16,32,128]{2,1,0:T(8,128)}, u32[]{:S(2)}) %copy-start) | copy-done | bytes 262168
  1.0 0.0 copy-start.1
  1.0 0.9 %copy-done.1 = s32[16,32,128]{2,1,0:T(8,128)S(1)} copy-done((s32[16,32,128]{2,1,0:T(8,128)S(1)}, s32[16,32,128]{2,1,0:T(8,128)}, u32[]{:S(2)}) %copy-start.1) | copy-done | bytes 262168
  1.9 0.0 copy-start.2
  1.9 0.7 copy-done.2
  2.6 0.0 copy-start.3
  2.6 0.7 copy-done.3
  3.2 68.0 %vcycle.1 = f32[16,32,128]{2,1,0:T(8,128)S(1)} custom-call(f32[16,32,128]{2,1,0:T(8,128)S(1)} %copy-done, s32[16,32,128]{2,1,0:T(8,128)S(1)} %copy-done.1, f32[8]{0:T(128)S(1)} %copy-done.2, f32[8]{0:T(128)S(1)} %copy-done.3), custom_call_target="tpu_custom_call" | custom-call | tf_op jit(solution)/shard_map/vcycle/pallas_call | solution.py:512
  71.2 0.7 copy.6
Async XLA Ops:
  0.0 0.9 %copy-start = (f32[16,32,128]{2,1,0:T(8,128)S(1)}, f32[16,32,128]{2,1,0:T(8,128)}, u32[]{:S(2)}) copy-start(f32[16,32,128]{2,1,0:T(8,128)} %src_ref.1) | copy-start | bytes 786436
  1.0 0.9 %copy-start.1 = (s32[16,32,128]{2,1,0:T(8,128)S(1)}, s32[16,32,128]{2,1,0:T(8,128)}, u32[]{:S(2)}) copy-start(s32[16,32,128]{2,1,0:T(8,128)} %tis_ref.1) | copy-start | bytes 786436
  1.9 0.7 copy-start.2
  2.6 0.7 copy-start.3

commit v2 on v1

v2 whole, which is shorter than its diff:
```python
import functools

import jax
import jax.numpy as jnp
from jax import lax
from jax.experimental import pallas as pl
from jax.experimental.pallas import tpu as pltpu
from jax.sharding import PartitionSpec as P

MESH = pl.DeviceIdType.MESH
F32 = jnp.float32
LEVELS = 6
TYPES = 8
HZ = 0.5 * 0.015625
REACH = (3, 4, 5, 5, 5, 5)


class Level:
    def __init__(self, index, rows, columns, across, most):
        self.index, self.rows, self.columns, self.across, self.most = index, rows, columns, across, most
        self.reach = REACH[index]
        self.ox = self.reach + 1
        self.nx = rows + 2 * self.ox + 2
        if across:
            self.oy = 8
            self.wide = self.mid = self.core = (8, columns)
            self.ny = 8 + columns + 8
        else:
            self.oy = 12
            self.core = (12, columns)
            around = -(-(columns + 8) // 8) * 8
            self.mid = (8, around)
            self.wide = (8, around) if self.reach < 5 else (4, around + 8)
            self.ny = around + 16
        self.own_x = pl.ds(self.ox, rows)
        self.own_y = pl.ds(self.oy, columns)
        self.half = 0.5 * 0.25**index

    def shape(self, *lead):
        return (*lead, self.nx, self.ny, 128)

    def span(self, radius):
        count = self.rows + 2 * radius
        times = -(-count // self.most)
        return self.ox - radius, -(-count // times), times


def overlap(size, step, radius, known):
    if known:
        low, high = {1: (-radius, -known), 0: (-known, size + known), -1: (size + known, size + radius)}[step]
        return low + step * size, low, high - low
    low = max(-radius, -step * size)
    high = min(size + radius, (1 - step) * size)
    return low + step * size, low, high - low


def kernel(sizes, levels, src_ref, tis_ref, dif_ref, upt_ref, out_ref, *scratch):
    gx_count, gy_count = sizes
    names = iter(scratch)
    tis = next(names)
    coef = [next(names) for _ in levels]
    right = [next(names) for _ in levels]
    wgt = [next(names) for _ in levels]
    inv = [next(names) for _ in levels]
    dia = [next(names) for _ in levels]
    one = [next(names) for _ in levels]
    two = [next(names) for _ in levels]
    tri = [next(names) for _ in levels]
    gat_c, gat_b = next(names), next(names)
    dif, upt = next(names), next(names)
    local_sem, send_sem, recv_sem = next(names), next(names), next(names)

    gx = lax.axis_index("gx")
    gy = lax.axis_index("gy")
    parity = lax.rem(gx, 2)
    places = {}

    def device(dx, dy):
        if ("x", dx) not in places:
            places["x", dx] = lax.rem(gx + (dx + gx_count), gx_count) if dx else gx
        if ("y", dy) not in places:
            places["y", dy] = lax.rem(gy + (dy + gy_count), gy_count) if dy else gy
        return places["x", dx], places["y", dy]

    counter = [0]

    def remote(source, target, dx, dy):
        number = counter[0]
        counter[0] += 1
        copy = pltpu.make_async_remote_copy(
            src_ref=source,
            dst_ref=target,
            send_sem=send_sem.at[number],
            recv_sem=recv_sem.at[number],
            device_id=device(dx, dy),
            device_id_type=MESH,
        )
        copy.start()
        return copy

    def arrived(copies):
        for copy in copies:
            copy.wait_recv()

    def left(copies):
        for copy in copies:
            copy.wait_send()

    def around(level, radius, known=0):
        far = -(-(radius - known) // level.rows)
        return [(dx, dy) for dx in range(-far, far + 1) for dy in (-1, 0, 1) if (dx, dy) != (0, 0)]

    def send_block(ref, level, radius, lead=(), known=0):
        copies = []
        for dx, dy in sorted(around(level, radius, known), key=lambda step: -abs(step[0]) - abs(step[1])):
            sx, tx, cx = overlap(level.rows, dx, radius, known)
            sy, ty, cy = overlap(level.columns, dy, radius, known)
            source = ref.at[(*lead, pl.ds(level.ox + sx, cx), pl.ds(level.oy + sy, cy))]
            target = ref.at[(*lead, pl.ds(level.ox + tx, cx), pl.ds(level.oy + ty, cy))]
            copies.append(remote(source, target, dx, dy))
        return copies

    def send_rows(ref, level, radius, lead=(), stride=1):
        copies = []
        far = -(-radius // level.rows)
        for step in range(1, far + 1):
            for dx in (step, -step):
                sx, tx, cx = overlap(level.rows, dx, radius, 0)
                source = ref.at[(*lead, pl.ds(level.ox + sx, cx), level.own_y)]
                target = ref.at[(*lead, pl.ds(level.ox + tx, cx), level.own_y)]
                copies.append(remote(source, target, dx * stride, 0))
        return copies

    def send_known(ref, level, moves, stride=1):
        copies = []
        for step, sx, tx, cx in moves:
            source = ref.at[pl.ds(level.ox + sx, cx), level.own_y]
            target = ref.at[pl.ds(level.ox + tx, cx), level.own_y]
            copies.append(remote(source, target, step * stride, 0))
        return copies

    def send_columns(ref):
        return [remote(ref.at[gy], ref.at[gy], 0, dy) for dy in range(1, gy_count)]

    def loop(count, step):
        def body(i, carry):
            step(i)
            return carry

        lax.fori_loop(0, count, body, 0)

    def seam(level, shape, axis, start, last):
        if axis == 0:
            half = level.index == LEVELS - 1
            total = level.rows * (gx_count // 2 if half else gx_count)
            base = (gx // 2 if half else gx) * level.rows + start - level.ox
        else:
            total = level.columns * gy_count
            base = gy * level.columns + start - level.oy
        place = lax.broadcasted_iota(jnp.int32, shape, axis) + base
        if last:
            return (place == total - 1) | (place == -1)
        return (place == 0) | (place == total)

    def types(x, blk, y, cy):
        kind = tis[pl.ds(x, blk), pl.ds(y, cy), :]
        kappa = jnp.full(kind.shape, dif[0], F32)
        sigma = jnp.full(kind.shape, upt[0], F32)
        for index in range(1, TYPES):
            hit = kind == index
            kappa = jnp.where(hit, dif[index], kappa)
            sigma = jnp.where(hit, upt[index], sigma)
        coef[0][0, pl.ds(x, blk), pl.ds(y, cy), :] = kappa
        coef[0][1, pl.ds(x, blk), pl.ds(y, cy), :] = sigma

    def mean(ref, lead, x, y, count):
        even = pl.ds(y, count, stride=2)
        odd = pl.ds(y + 1, count, stride=2)
        near = ref[(*lead, x, even, slice(None))] + ref[(*lead, x + 1, even, slice(None))]
        far = ref[(*lead, x, odd, slice(None))] + ref[(*lead, x + 1, odd, slice(None))]
        return 0.25 * (near + far)

    def weights(level, rows=None, columns=None, start=False):
        index = level.index
        first, blk, times = rows or level.span(level.reach)
        y, cy = columns or level.wide
        half = level.half

        def step(i):
            x = first + i * blk
            here = (pl.ds(x, blk), pl.ds(y, cy), slice(None))
            field = coef[index].at[0]
            centre = field[here]
            plane = lax.broadcasted_iota(jnp.int32, centre.shape, 2)
            row, column = pl.ds(x, blk), pl.ds(y, cy)
            faces = [
                (half, field[pl.ds(x + 1, blk), column, :], seam(level, centre.shape, 0, x, True)),
                (half, field[pl.ds(x - 1, blk), column, :], seam(level, centre.shape, 0, x, False)),
            ]
            if level.across:
                faces += [
                    (half, field[row, pl.ds(y + 1, cy), :], None),
                    (half, field[row, pl.ds(y - 1, cy), :], None),
                ]
            else:
                faces += [
                    (half, field[row, pl.ds(y + 1, cy), :], seam(level, centre.shape, 1, y, True)),
                    (half, field[row, pl.ds(y - 1, cy), :], seam(level, centre.shape, 1, y, False)),
                ]
            faces += [
                (HZ, pltpu.roll(centre, 127, 2), plane == 127),
                (HZ, pltpu.roll(centre, 1, 2), plane == 0),
            ]
            diag = coef[index][(1, *here)]
            weight = []
            for scale, beyond, closed in faces:
                if closed is not None:
                    beyond = jnp.where(closed, 0.0, beyond)
                face = scale * (centre + beyond)
                diag = diag + face
                weight.append(face)
            inverse = 0.8 / diag
            dia[index][here] = 1.25 * diag
            if start:
                one[index][here] = inverse * right[index][here]
            else:
                inv[index][here] = inverse
            for number, (scale, beyond, closed) in enumerate(faces):
                value = inverse * weight[number]
                if closed is not None:
                    value = jnp.where(closed, 0.0, value)
                wgt[index][(number, *here)] = value

        loop(times, step)

    def pulled(level, field, x, blk, y, cy, centre):
        index = level.index
        here = (pl.ds(x, blk), pl.ds(y, cy), slice(None))
        weight = wgt[index]
        total = one[index][here] + weight[(0, *here)] * field[pl.ds(x + 1, blk), pl.ds(y, cy), :]
        other = weight[(1, *here)] * field[pl.ds(x - 1, blk), pl.ds(y, cy), :]
        total = total + weight[(2, *here)] * field[pl.ds(x, blk), pl.ds(y + 1, cy), :]
        other = other + weight[(3, *here)] * field[pl.ds(x, blk), pl.ds(y - 1, cy), :]
        total = total + weight[(4, *here)] * pltpu.roll(centre, 127, 2)
        other = other + weight[(5, *here)] * pltpu.roll(centre, 1, 2)
        return total + other

    def first_sweep(level):
        index = level.index
        first, blk, times = level.span(level.reach)

        def step(i):
            here = (pl.ds(first + i * blk, blk), pl.ds(*level.wide), slice(None))
            one[index][here] = inv[index][here] * right[index][here]

        loop(times, step)

    def sweep(level, source, target, radius):
        first, blk, times = level.span(radius)
        y, cy = level.mid if radius else level.core

        def step(i):
            x = first + i * blk
            here = (pl.ds(x, blk), pl.ds(y, cy), slice(None))
            centre = source[here]
            target[here] = 0.2 * centre + pulled(level, source, x, blk, y, cy, centre)

        loop(times, step)

    def residual(level, radius, columns):
        index = level.index
        first, blk, times = level.span(radius)
        y, cy = columns

        def step(i):
            x = first + i * blk
            here = (pl.ds(x, blk), pl.ds(y, cy), slice(None))
            centre = two[index][here]
            total = pulled(level, two[index], x, blk, y, cy, centre)
            tri[index][here] = dia[index][here] * (total - 0.8 * centre)

        loop(times, step)

    def lift(value, level, x, y, count):
        for row in (x, x + 1):
            for column in (y, y + 1):
                spot = (row, pl.ds(column, count, stride=2), slice(None))
                two[level.index][spot] = two[level.index][spot] + value

    zero, one_, two_, three, four, five = levels

    loads = []
    for position, (source, target) in enumerate(
        (
            (tis_ref, tis.at[zero.own_x, zero.own_y]),
            (src_ref, right[0].at[zero.own_x, zero.own_y]),
            (dif_ref, dif),
            (upt_ref, upt),
        )
    ):
        copy = pltpu.make_async_copy(source, target, local_sem.at[position])
        copy.start()
        loads.append(copy)
    barrier = pltpu.get_barrier_semaphore()
    greeted = around(two_, two_.reach + 1)
    greeted = greeted + [(0, dy) for dy in range(2, gy_count - 1)]
    for dx, dy in greeted:
        pl.semaphore_signal(barrier, inc=1, device_id=device(dx, dy), device_id_type=MESH)
    for level in (three, four, five):
        index = level.index
        for ref in (coef[index].at[0], one[index], two[index], tri[index]):
            ref[:, pl.ds(0, 8), :] = jnp.zeros((level.nx, 8, 128), F32)
            ref[:, pl.ds(8 + level.columns, 8), :] = jnp.zeros((level.nx, 8, 128), F32)
    for copy in loads:
        copy.wait()
    pl.semaphore_wait(barrier, len(greeted))

    sent_tis = send_block(tis, zero, zero.reach + 1)
    sent_src = send_block(right[0], zero, zero.reach)
    loop(zero.rows // 2, lambda i: types(zero.ox + 2 * i, 2, zero.oy, zero.columns))

    def coarsen(ref, lead, fine, level, field):
        def step(i):
            value = mean(ref, lead, fine.ox + 2 * i, fine.oy, level.columns)
            coef[level.index][field, level.ox + i, level.own_y, :] = value

        loop(level.rows, step)

    coarsen(coef[0], (0,), zero, one_, 0)
    coarsen(coef[0], (1,), zero, one_, 1)
    sent_c1 = send_block(coef[1], one_, one_.reach + 1, (slice(None),))
    for field in (0, 1):
        coarsen(coef[1], (field,), one_, two_, field)
    sent_c2 = send_block(coef[2], two_, two_.reach + 1, (slice(None),))
    for field in (0, 1):
        for row in (0, 1):
            gat_c[gy, field, row] = mean(coef[2], (field,), two_.ox + 2 * row, two_.oy, 4)
    sent_c3 = send_columns(gat_c)
    weights(zero, (zero.ox + 1, (zero.rows - 2) // 2, 2), zero.core, True)

    arrived(sent_tis)
    ring = zero.reach + 1
    types(zero.ox - ring, ring, 8, zero.mid[1])
    types(zero.ox + zero.rows, ring, 8, zero.mid[1])
    loop(zero.rows // 8, lambda i: types(zero.ox + 8 * i, 8, 8, ring))
    loop(zero.rows // 8, lambda i: types(zero.ox + 8 * i, 8, zero.oy + zero.columns, ring))
    arrived(sent_src)
    weights(zero, (zero.ox - zero.reach, zero.reach + 1, 1), zero.wide, True)
    weights(zero, (zero.ox + zero.rows - 1, zero.reach + 1, 1), zero.wide, True)
    weights(zero, (zero.ox + 1, (zero.rows - 2) // 2, 2), (8, 8), True)
    weights(zero, (zero.ox + 1, (zero.rows - 2) // 2, 2), (zero.oy + zero.columns - 4, 8), True)

    def restrict_to(fine, level, known):
        def step(i):
            value = mean(tri[fine.index], (), fine.ox + 2 * (i - known), fine.oy - 2 * known, level.columns + 2 * known)
            right[level.index][level.ox - known + i, pl.ds(level.oy - known, level.columns + 2 * known), :] = value

        loop(level.rows + 2 * known, step)

    sweep(zero, one[0], two[0], zero.reach - 1)
    residual(zero, 0, zero.core)
    restrict_to(zero, one_, 0)
    sent_b1 = send_block(right[1], one_, one_.reach)
    left(sent_tis)
    left(sent_src)
    arrived(sent_c1)
    weights(one_)

    arrived(sent_b1)
    first_sweep(one_)
    sweep(one_, one[1], two[1], one_.reach - 1)
    residual(one_, 2, one_.mid)
    restrict_to(one_, two_, 1)
    sent_b2 = send_block(right[2], two_, two_.reach, (), 1)
    arrived(sent_c2)
    weights(two_)
    arrived(sent_c3)

    def unpack(rows, read, write):
        for part in range(gy_count):
            for row in range(rows):
                write(row, pl.ds(8 + 4 * part, 4), read(part, row))

    for field in (0, 1):

        def write(row, columns, value):
            coef[3][field, three.ox + row, columns, :] = value

        unpack(2, lambda part, row: gat_c[part, field, row], write)
    sent_x3 = send_rows(coef[3], three, three.reach + 1, (slice(None),))
    for field in (0, 1):
        coef[4][field, four.ox, four.own_y, :] = mean(coef[3], (field,), three.ox, 8, four.columns)
    left(sent_c1)
    left(sent_c2)
    left(sent_c3)
    left(sent_b1)

    arrived(sent_b2)
    first_sweep(two_)
    sweep(two_, one[2], two[2], two_.reach - 1)
    residual(two_, 2, two_.core)
    for row in range(4):
        gat_b[gy, row] = mean(tri[2], (), two_.ox - 2 + 2 * row, two_.oy, 4)
    sent_b3 = send_columns(gat_b)
    arrived(sent_x3)
    sent_c4 = send_rows(coef[4], four, four.reach + 1, (slice(None),))
    weights(three)
    left(sent_b2)

    arrived(sent_b3)

    def write_right(row, columns, value):
        right[3][three.ox - 1 + row, columns, :] = value

    unpack(4, lambda part, row: gat_b[part, row], write_right)
    sent_r3 = send_known(right[3], three, ((2, -1, -5, 4), (-2, -1, 3, 4)))
    arrived(sent_c4)
    chip = four.ox - parity
    for field in (0, 1):
        coef[5][field, five.ox, five.own_y, :] = mean(coef[4], (field,), chip, 8, five.columns)
    sent_c5 = send_rows(coef[5], five, five.reach + 1, (slice(None),), 2)
    weights(four)
    left(sent_x3)
    left(sent_b3)
    left(sent_c4)
    arrived(sent_r3)
    first_sweep(three)
    sweep(three, one[3], two[3], three.reach - 1)
    residual(three, 2, three.core)
    for row in (-1, 0, 1):
        right[4][four.ox + row, four.own_y, :] = mean(tri[3], (), three.ox + 2 * row, 8, four.columns)

    moves = ((4, -1, -5, 1), (-4, 1, 5, 1), (3, -1, -4, 3), (-3, -1, 2, 3))
    sent_r4 = send_known(right[4], four, moves)
    arrived(sent_c5)
    weights(five)
    left(sent_r3)
    left(sent_c5)
    arrived(sent_r4)
    first_sweep(four)
    sweep(four, one[4], two[4], four.reach - 1)
    residual(four, 3, four.core)
    for row in (-1, 0, 1):
        right[5][five.ox + row, five.own_y, :] = mean(tri[4], (), chip + 2 * row, 8, five.columns)

    sent_r5 = send_known(right[5], five, moves, 2)
    left(sent_r4)
    arrived(sent_r5)
    first_sweep(five)
    sweep(five, one[5], two[5], 4)
    sweep(five, two[5], tri[5], 3)
    sweep(five, tri[5], two[5], 2)
    left(sent_r5)

    def ascend(level, last):
        index = level.index
        sweep(level, two[index], tri[index], last + 1)
        sweep(level, tri[index], two[index], last)

    for offset in range(-4, 5):
        row = five.ox - 4 + (parity + (offset + 8)) // 2
        value = two[5][row, five.own_y, :]
        for column in (8, 9):
            spot = (four.ox + offset, pl.ds(column, five.columns, stride=2), slice(None))
            two[4][spot] = two[4][spot] + value
    ascend(four, 2)
    for offset in range(-2, 3):
        lift(two[4][four.ox + offset, four.own_y, :], three, three.ox + 2 * offset, 8, four.columns)
    ascend(three, 2)
    for offset in range(-2, 4):
        value = two[3][three.ox + offset, pl.ds(6 + 4 * gy, 8), :]
        lift(value, two_, two_.ox + 2 * offset, two_.oy - 4, 8)
    ascend(two_, 2)

    def lift_one(i):
        value = two[2][two_.ox - 2 + i, pl.ds(two_.oy - 2, two_.columns + 4), :]
        lift(value, one_, one_.ox - 4 + 2 * i, one_.oy - 4, two_.columns + 4)

    loop(two_.rows + 4, lift_one)
    ascend(one_, 1)

    def lift_zero(i):
        value = two[1][one_.ox - 1 + i, pl.ds(one_.oy - 1, one_.columns + 2), :]
        lift(value, zero, zero.ox - 2 + 2 * i, zero.oy - 2, one_.columns + 2)

    loop(one_.rows + 2, lift_zero)
    sweep(zero, two[0], tri[0], 1)
    y, cy = zero.core
    part = zero.rows // 4
    copies = []
    for chunk in range(4):
        x = zero.ox + chunk * part
        here = (pl.ds(x, part), pl.ds(y, cy), slice(None))
        centre = tri[0][here]
        two[0][here] = 0.2 * centre + pulled(zero, tri[0], x, part, y, cy, centre)
        copy = pltpu.make_async_copy(
            two[0].at[pl.ds(x, part), pl.ds(y, cy)], out_ref.at[pl.ds(chunk * part, part)], local_sem.at[chunk]
        )
        copy.start()
        copies.append(copy)
    for copy in copies:
        copy.wait()


def build(mesh, rows, columns):
    gx_count, gy_count = mesh.shape["gx"], mesh.shape["gy"]
    levels = [
        Level(0, rows, columns, False, 5),
        Level(1, rows // 2, columns // 2, False, 7),
        Level(2, rows // 4, columns // 4, False, 12),
        Level(3, rows // 8, columns // 8 * gy_count, True, 6),
        Level(4, rows // 16, columns // 16 * gy_count, True, 11),
        Level(5, 1, columns // 32 * gy_count, True, 11),
    ]
    zero = levels[0]
    messages = 160
    scratch = [pltpu.VMEM(zero.shape(), jnp.int32)]
    scratch += [pltpu.VMEM(level.shape(2), F32) for level in levels]
    scratch += [pltpu.VMEM(level.shape(), F32) for level in levels]
    scratch += [pltpu.VMEM(level.shape(6), F32) for level in levels]
    for _ in range(5):
        scratch += [pltpu.VMEM(level.shape(), F32) for level in levels]
    scratch += [
        pltpu.VMEM((gy_count, 2, 2, 4, 128), F32),
        pltpu.VMEM((gy_count, 4, 4, 128), F32),
        pltpu.SMEM((TYPES,), F32),
        pltpu.SMEM((TYPES,), F32),
        pltpu.SemaphoreType.DMA((4,)),
        pltpu.SemaphoreType.DMA((messages,)),
        pltpu.SemaphoreType.DMA((messages,)),
    ]
    return pl.pallas_call(
        functools.partial(kernel, (gx_count, gy_count), levels),
        out_shape=jax.ShapeDtypeStruct((rows, columns, 128), F32),
        in_specs=[
            pl.BlockSpec(memory_space=pltpu.HBM),
            pl.BlockSpec(memory_space=pltpu.HBM),
            pl.BlockSpec(memory_space=pltpu.HBM),
            pl.BlockSpec(memory_space=pltpu.HBM),
        ],
        out_specs=pl.BlockSpec(memory_space=pltpu.HBM),
        scratch_shapes=scratch,
        name="vcycle",
        compiler_params=pltpu.CompilerParams(
            collective_id=0, has_side_effects=True, vmem_limit_bytes=64 * 2**20
        ),
    )


def solution(mesh):
    def body(source, tissue, diffusivity, uptake):
        call = build(mesh, source.shape[0], source.shape[1])
        return call(source, tissue, diffusivity, uptake)

    in_specs = (P("gx", "gy", None), P("gx", "gy", None), P(), P())
    out_specs = P("gx", "gy", None)
    return jax.shard_map(body, mesh=mesh, in_specs=in_specs, out_specs=out_specs, check_vma=False)
```

time: 72.1 us -> 62.3 us (0.86)
  Pallas kernels: 68 us -> 60 us
  local copies, waits for them, and re-layouts: 3.91 us -> 1.67 us
    pallas_call x1, Pallas kernels: 68 us -> 60 us  [body(): return call(source, tissue, diffusivity, uptake)]
    unnamed x9 -> x1, local copies, waits for them, and re-layouts: 3.91 us -> 1.67 us
where the time goes in v2:
time: 62.3 us; the launch traced here: 61.7 us
  Pallas kernels  60 us (96%)
  local copies, waits for them, and re-layouts  1.67 us (3%)
    pallas_call x1, Pallas kernels, body(): return call(source, tissue, diffusivity, uptake)  60 us
    unnamed x1, local copies, waits for them, and re-layouts  1.67 us

profile of v2, /device:TPU:1, one launch (start us, length us, event | category | flops | bytes accessed | tf_op | source)
XLA Modules:
  0.0 61.7 jit_solution(1549788310726330246)
XLA Ops:
  0.0 60.0 %vcycle.1 = f32[16,32,128]{2,1,0:T(8,128)} custom-call(f32[16,32,128]{2,1,0:T(8,128)} %src_ref.1, s32[16,32,128]{2,1,0:T(8,128)} %tis_ref.1, f32[8]{0:T(128)} %dif_ref.1, f32[8]{0:T(128)} %upt_ref.1), custom_call_target="tpu_custom_call" | custom-call | tf_op jit(solution)/shard_map/vcycle/pallas_call | solution.py:553
  60.0 1.7 %copy.6 = f32[16,32,128]{2,1,0:T(8,128)} copy(f32[16,32,128]{2,1,0:T(8,128)} %vcycle.1) | data formatting | bytes 524288

commit v3 on v2

--- a/solution.py
+++ b/solution.py
@@ -110,32 +110,24 @@
         far = -(-(radius - known) // level.rows)
         return [(dx, dy) for dx in range(-far, far + 1) for dy in (-1, 0, 1) if (dx, dy) != (0, 0)]
 
-    def send_block(ref, level, radius, lead=(), known=0):
+    def send_block(ref, level, radius, lead=(), known=0, origin=None):
         copies = []
         for dx, dy in sorted(around(level, radius, known), key=lambda step: -abs(step[0]) - abs(step[1])):
             sx, tx, cx = overlap(level.rows, dx, radius, known)
             sy, ty, cy = overlap(level.columns, dy, radius, known)
-            source = ref.at[(*lead, pl.ds(level.ox + sx, cx), pl.ds(level.oy + sy, cy))]
+            if origin is None:
+                source = ref.at[(*lead, pl.ds(level.ox + sx, cx), pl.ds(level.oy + sy, cy))]
+            else:
+                source = origin.at[pl.ds(sx, cx), pl.ds(sy, cy)]
             target = ref.at[(*lead, pl.ds(level.ox + tx, cx), pl.ds(level.oy + ty, cy))]
             copies.append(remote(source, target, dx, dy))
         return copies
 
-    def send_rows(ref, level, radius, lead=(), stride=1):
-        copies = []
-        far = -(-radius // level.rows)
-        for step in range(1, far + 1):
-            for dx in (step, -step):
-                sx, tx, cx = overlap(level.rows, dx, radius, 0)
-                source = ref.at[(*lead, pl.ds(level.ox + sx, cx), level.own_y)]
-                target = ref.at[(*lead, pl.ds(level.ox + tx, cx), level.own_y)]
-                copies.append(remote(source, target, dx * stride, 0))
-        return copies
-
-    def send_known(ref, level, moves, stride=1):
+    def send_known(ref, level, moves, stride=1, lead=()):
         copies = []
         for step, sx, tx, cx in moves:
-            source = ref.at[pl.ds(level.ox + sx, cx), level.own_y]
-            target = ref.at[pl.ds(level.ox + tx, cx), level.own_y]
+            source = ref.at[(*lead, pl.ds(level.ox + sx, cx), level.own_y)]
+            target = ref.at[(*lead, pl.ds(level.ox + tx, cx), level.own_y)]
             copies.append(remote(source, target, step * stride, 0))
         return copies
 
@@ -289,6 +281,10 @@
 
     zero, one_, two_, three, four, five = levels
 
+    barrier = pltpu.get_barrier_semaphore()
+    greeted = around(zero, zero.reach + 1) + ([(0, 2), (0, -2)] if gy_count > 4 else [])
+    for dx, dy in greeted:
+        pl.semaphore_signal(barrier, inc=1, device_id=device(dx, dy), device_id_type=MESH)
     loads = []
     for position, (source, target) in enumerate(
         (
@@ -301,11 +297,10 @@
         copy = pltpu.make_async_copy(source, target, local_sem.at[position])
         copy.start()
         loads.append(copy)
-    barrier = pltpu.get_barrier_semaphore()
-    greeted = around(two_, two_.reach + 1)
-    greeted = greeted + [(0, dy) for dy in range(2, gy_count - 1)]
-    for dx, dy in greeted:
-        pl.semaphore_signal(barrier, inc=1, device_id=device(dx, dy), device_id_type=MESH)
+    pl.semaphore_wait(barrier, len(greeted))
+
+    sent_tis = send_block(tis, zero, zero.reach + 1, (), 0, tis_ref)
+    sent_src = send_block(right[0], zero, zero.reach, (), 0, src_ref)
     for level in (three, four, five):
         index = level.index
         for ref in (coef[index].at[0], one[index], two[index], tri[index]):
@@ -313,29 +308,27 @@
             ref[:, pl.ds(8 + level.columns, 8), :] = jnp.zeros((level.nx, 8, 128), F32)
     for copy in loads:
         copy.wait()
-    pl.semaphore_wait(barrier, len(greeted))
-
-    sent_tis = send_block(tis, zero, zero.reach + 1)
-    sent_src = send_block(right[0], zero, zero.reach)
     loop(zero.rows // 2, lambda i: types(zero.ox + 2 * i, 2, zero.oy, zero.columns))
 
-    def coarsen(ref, lead, fine, level, field):
-        def step(i):
-            value = mean(ref, lead, fine.ox + 2 * i, fine.oy, level.columns)
-            coef[level.index][field, level.ox + i, level.own_y, :] = value
-
-        loop(level.rows, step)
-
-    coarsen(coef[0], (0,), zero, one_, 0)
-    coarsen(coef[0], (1,), zero, one_, 1)
-    sent_c1 = send_block(coef[1], one_, one_.reach + 1, (slice(None),))
-    for field in (0, 1):
-        coarsen(coef[1], (field,), one_, two_, field)
-    sent_c2 = send_block(coef[2], two_, two_.reach + 1, (slice(None),))
-    for field in (0, 1):
-        for row in (0, 1):
-            gat_c[gy, field, row] = mean(coef[2], (field,), two_.ox + 2 * row, two_.oy, 4)
-    sent_c3 = send_columns(gat_c)
+    def coarsen(fine, level, known):
+        for field in (0, 1):
+
+            def step(i):
+                value = mean(
+                    coef[fine.index],
+                    (field,),
+                    fine.ox + 2 * (i - known),
+                    fine.oy - 2 * known,
+                    level.columns + 2 * known,
+                )
+                here = (level.ox - known + i, pl.ds(level.oy - known, level.columns + 2 * known), slice(None))
+                coef[level.index][(field, *here)] = value
+
+            loop(level.rows + 2 * known, step)
+
+    coarsen(zero, one_, 0)
+    both = (slice(None),)
+    sent_c1 = send_block(coef[1], one_, one_.reach + 1, both)
     weights(zero, (zero.ox + 1, (zero.rows - 2) // 2, 2), zero.core, True)
 
     arrived(sent_tis)
@@ -364,7 +357,10 @@
     left(sent_tis)
     left(sent_src)
     arrived(sent_c1)
+    coarsen(one_, two_, 2)
+    sent_c2 = send_block(coef[2], two_, two_.reach + 1, both, 2)
     weights(one_)
+    left(sent_c1)
 
     arrived(sent_b1)
     first_sweep(one_)
@@ -373,26 +369,12 @@
     restrict_to(one_, two_, 1)
     sent_b2 = send_block(right[2], two_, two_.reach, (), 1)
     arrived(sent_c2)
+    for field in (0, 1):
+        for row in range(4):
+            gat_c[gy, field, row] = mean(coef[2], (field,), two_.ox - 2 + 2 * row, two_.oy, 4)
+    sent_c3 = send_columns(gat_c)
     weights(two_)
-    arrived(sent_c3)
-
-    def unpack(rows, read, write):
-        for part in range(gy_count):
-            for row in range(rows):
-                write(row, pl.ds(8 + 4 * part, 4), read(part, row))
-
-    for field in (0, 1):
-
-        def write(row, columns, value):
-            coef[3][field, three.ox + row, columns, :] = value
-
-        unpack(2, lambda part, row: gat_c[part, field, row], write)
-    sent_x3 = send_rows(coef[3], three, three.reach + 1, (slice(None),))
-    for field in (0, 1):
-        coef[4][field, four.ox, four.own_y, :] = mean(coef[3], (field,), three.ox, 8, four.columns)
-    left(sent_c1)
     left(sent_c2)
-    left(sent_c3)
     left(sent_b1)
 
     arrived(sent_b2)
@@ -402,27 +384,40 @@
     for row in range(4):
         gat_b[gy, row] = mean(tri[2], (), two_.ox - 2 + 2 * row, two_.oy, 4)
     sent_b3 = send_columns(gat_b)
-    arrived(sent_x3)
-    sent_c4 = send_rows(coef[4], four, four.reach + 1, (slice(None),))
-    weights(three)
+
+    def unpack(read, write):
+        for part in range(gy_count):
+            for row in range(4):
+                write(row, pl.ds(8 + 4 * part, 4), read(part, row))
+
+    arrived(sent_c3)
+    for field in (0, 1):
+
+        def write(row, columns, value):
+            coef[3][field, three.ox - 1 + row, columns, :] = value
+
+        unpack(lambda part, row: gat_c[part, field, row], write)
+    moves = ((2, -1, -5, 4), (-2, -1, 3, 4))
+    sent_x3 = send_known(coef[3], three, (*moves, (3, 0, -6, 1), (-3, 1, 7, 1)), 1, both)
     left(sent_b2)
+    left(sent_c3)
 
     arrived(sent_b3)
 
     def write_right(row, columns, value):
         right[3][three.ox - 1 + row, columns, :] = value
 
-    unpack(4, lambda part, row: gat_b[part, row], write_right)
-    sent_r3 = send_known(right[3], three, ((2, -1, -5, 4), (-2, -1, 3, 4)))
-    arrived(sent_c4)
-    chip = four.ox - parity
-    for field in (0, 1):
-        coef[5][field, five.ox, five.own_y, :] = mean(coef[4], (field,), chip, 8, five.columns)
-    sent_c5 = send_rows(coef[5], five, five.reach + 1, (slice(None),), 2)
-    weights(four)
+    unpack(lambda part, row: gat_b[part, row], write_right)
+    sent_r3 = send_known(right[3], three, moves)
+    arrived(sent_x3)
+    for row in range(-3, 4):
+        for field in (0, 1):
+            value = mean(coef[3], (field,), three.ox + 2 * row, 8, four.columns)
+            coef[4][field, four.ox + row, four.own_y, :] = value
+    sent_c4 = send_known(coef[4], four, ((3, -3, -6, 3), (-3, 1, 4, 3)), 1, both)
+    weights(three)
     left(sent_x3)
     left(sent_b3)
-    left(sent_c4)
     arrived(sent_r3)
     first_sweep(three)
     sweep(three, one[3], two[3], three.reach - 1)
@@ -432,10 +427,16 @@
 
     moves = ((4, -1, -5, 1), (-4, 1, 5, 1), (3, -1, -4, 3), (-3, -1, 2, 3))
     sent_r4 = send_known(right[4], four, moves)
-    arrived(sent_c5)
-    weights(five)
+    arrived(sent_c4)
+    chip = four.ox - parity
+    for row in range(-2, 3):
+        for field in (0, 1):
+            value = mean(coef[4], (field,), chip + 2 * row, 8, five.columns)
+            coef[5][field, five.ox + row, five.own_y, :] = value
+    sent_c5 = send_known(coef[5], five, ((4, -2, -6, 4), (-4, -1, 3, 4)), 2, both)
+    weights(four)
     left(sent_r3)
-    left(sent_c5)
+    left(sent_c4)
     arrived(sent_r4)
     first_sweep(four)
     sweep(four, one[4], two[4], four.reach - 1)
@@ -444,7 +445,10 @@
         right[5][five.ox + row, five.own_y, :] = mean(tri[4], (), chip + 2 * row, 8, five.columns)
 
     sent_r5 = send_known(right[5], five, moves, 2)
+    arrived(sent_c5)
+    weights(five)
     left(sent_r4)
+    left(sent_c5)
     arrived(sent_r5)
     first_sweep(five)
     sweep(five, one[5], two[5], 4)
@@ -513,7 +517,7 @@
         Level(5, 1, columns // 32 * gy_count, True, 11),
     ]
     zero = levels[0]
-    messages = 160
+    messages = 96
     scratch = [pltpu.VMEM(zero.shape(), jnp.int32)]
     scratch += [pltpu.VMEM(level.shape(2), F32) for level in levels]
     scratch += [pltpu.VMEM(level.shape(), F32) for level in levels]
@@ -521,7 +525,7 @@
     for _ in range(5):
         scratch += [pltpu.VMEM(level.shape(), F32) for level in levels]
     scratch += [
-        pltpu.VMEM((gy_count, 2, 2, 4, 128), F32),
+        pltpu.VMEM((gy_count, 2, 4, 4, 128), F32),
         pltpu.VMEM((gy_count, 4, 4, 128), F32),
         pltpu.SMEM((TYPES,), F32),
         pltpu.SMEM((TYPES,), F32),

time: 62.3 us -> 59.4 us (0.953)
  Pallas kernels: 60 us -> 57.6 us
    pallas_call x1, Pallas kernels: 60 us -> 57.6 us  [body(): return call(source, tissue, diffusivity, uptake)]
where the time goes in v3:
time: 59.4 us; the launch traced here: 59.3 us
  Pallas kernels  57.6 us (97%)
  local copies, waits for them, and re-layouts  1.67 us (3%)
    pallas_call x1, Pallas kernels, body(): return call(source, tissue, diffusivity, uptake)  57.6 us
    unnamed x1, local copies, waits for them, and re-layouts  1.67 us

profile of v3, /device:TPU:1, one launch (start us, length us, event | category | flops | bytes accessed | tf_op | source)
XLA Modules:
  0.0 59.3 jit_solution(4046279175775676759)
XLA Ops:
  0.0 57.6 %vcycle.1 = f32[16,32,128]{2,1,0:T(8,128)} custom-call(f32[16,32,128]{2,1,0:T(8,128)} %src_ref.1, s32[16,32,128]{2,1,0:T(8,128)} %tis_ref.1, f32[8]{0:T(128)} %dif_ref.1, f32[8]{0:T(128)} %upt_ref.1), custom_call_target="tpu_custom_call" | custom-call | tf_op jit(solution)/shard_map/vcycle/pallas_call | solution.py:557
  57.6 1.7 %copy.6 = f32[16,32,128]{2,1,0:T(8,128)} copy(f32[16,32,128]{2,1,0:T(8,128)} %vcycle.1) | data formatting | bytes 524288

commit v4 on v3

--- a/solution.py
+++ b/solution.py
@@ -131,10 +131,25 @@
             copies.append(remote(source, target, step * stride, 0))
         return copies
 
-    def send_columns(ref):
-        return [remote(ref.at[gy], ref.at[gy], 0, dy) for dy in range(1, gy_count)]
-
-    def loop(count, step):
+    def send_columns(source, ref, level, moves, position, lead=()):
+        columns = pl.ds(8 + 4 * gy, 4)
+        target = ref.at[(*lead, pl.ds(level.ox - 1, 4), columns)]
+        own = pltpu.make_async_copy(source, target, local_sem.at[position])
+        own.start()
+        copies = []
+        for dy in sorted(range(gy_count), key=lambda step: -min(step, gy_count - step)):
+            for dx, tx in moves:
+                if dx or dy:
+                    target = ref.at[(*lead, pl.ds(level.ox + tx, 4), columns)]
+                    copies.append(remote(source, target, dx, dy))
+        return own, copies
+
+    def loop(count, step, unrolled=False):
+        if unrolled:
+            for i in range(count):
+                step(i)
+            return
+
         def body(i, carry):
             step(i)
             return carry
@@ -223,7 +238,7 @@
                     value = jnp.where(closed, 0.0, value)
                 wgt[index][(number, *here)] = value
 
-        loop(times, step)
+        loop(times, step, times < 3)
 
     def pulled(level, field, x, blk, y, cy, centre):
         index = level.index
@@ -245,7 +260,7 @@
             here = (pl.ds(first + i * blk, blk), pl.ds(*level.wide), slice(None))
             one[index][here] = inv[index][here] * right[index][here]
 
-        loop(times, step)
+        loop(times, step, True)
 
     def sweep(level, source, target, radius):
         first, blk, times = level.span(radius)
@@ -257,7 +272,7 @@
             centre = source[here]
             target[here] = 0.2 * centre + pulled(level, source, x, blk, y, cy, centre)
 
-        loop(times, step)
+        loop(times, step, True)
 
     def residual(level, radius, columns):
         index = level.index
@@ -271,7 +286,7 @@
             total = pulled(level, two[index], x, blk, y, cy, centre)
             tri[index][here] = dia[index][here] * (total - 0.8 * centre)
 
-        loop(times, step)
+        loop(times, step, True)
 
     def lift(value, level, x, y, count):
         for row in (x, x + 1):
@@ -335,20 +350,20 @@
     ring = zero.reach + 1
     types(zero.ox - ring, ring, 8, zero.mid[1])
     types(zero.ox + zero.rows, ring, 8, zero.mid[1])
-    loop(zero.rows // 8, lambda i: types(zero.ox + 8 * i, 8, 8, ring))
-    loop(zero.rows // 8, lambda i: types(zero.ox + 8 * i, 8, zero.oy + zero.columns, ring))
+    types(zero.ox, zero.rows, 8, ring)
+    types(zero.ox, zero.rows, zero.oy + zero.columns, ring)
     arrived(sent_src)
     weights(zero, (zero.ox - zero.reach, zero.reach + 1, 1), zero.wide, True)
     weights(zero, (zero.ox + zero.rows - 1, zero.reach + 1, 1), zero.wide, True)
-    weights(zero, (zero.ox + 1, (zero.rows - 2) // 2, 2), (8, 8), True)
-    weights(zero, (zero.ox + 1, (zero.rows - 2) // 2, 2), (zero.oy + zero.columns - 4, 8), True)
+    weights(zero, (zero.ox + 1, zero.rows - 2, 1), (8, 8), True)
+    weights(zero, (zero.ox + 1, zero.rows - 2, 1), (zero.oy + zero.columns - 4, 8), True)
 
     def restrict_to(fine, level, known):
         def step(i):
             value = mean(tri[fine.index], (), fine.ox + 2 * (i - known), fine.oy - 2 * known, level.columns + 2 * known)
             right[level.index][level.ox - known + i, pl.ds(level.oy - known, level.columns + 2 * known), :] = value
 
-        loop(level.rows + 2 * known, step)
+        loop(level.rows + 2 * known, step, True)
 
     sweep(zero, one[0], two[0], zero.reach - 1)
     residual(zero, 0, zero.core)
@@ -371,8 +386,8 @@
     arrived(sent_c2)
     for field in (0, 1):
         for row in range(4):
-            gat_c[gy, field, row] = mean(coef[2], (field,), two_.ox - 2 + 2 * row, two_.oy, 4)
-    sent_c3 = send_columns(gat_c)
+            gat_c[field, row] = mean(coef[2], (field,), two_.ox - 2 + 2 * row, two_.oy, 4)
+    own_c3, sent_c3 = send_columns(gat_c, coef[3], three, ((0, -1),), 0, both)
     weights(two_)
     left(sent_c2)
     left(sent_b1)
@@ -382,33 +397,14 @@
     sweep(two_, one[2], two[2], two_.reach - 1)
     residual(two_, 2, two_.core)
     for row in range(4):
-        gat_b[gy, row] = mean(tri[2], (), two_.ox - 2 + 2 * row, two_.oy, 4)
-    sent_b3 = send_columns(gat_b)
-
-    def unpack(read, write):
-        for part in range(gy_count):
-            for row in range(4):
-                write(row, pl.ds(8 + 4 * part, 4), read(part, row))
-
+        gat_b[row] = mean(tri[2], (), two_.ox - 2 + 2 * row, two_.oy, 4)
+
+    own_b3, sent_b3 = send_columns(gat_b, right[3], three, ((2, -5), (-2, 3), (0, -1)), 1)
+    own_c3.wait()
     arrived(sent_c3)
-    for field in (0, 1):
-
-        def write(row, columns, value):
-            coef[3][field, three.ox - 1 + row, columns, :] = value
-
-        unpack(lambda part, row: gat_c[part, field, row], write)
-    moves = ((2, -1, -5, 4), (-2, -1, 3, 4))
-    sent_x3 = send_known(coef[3], three, (*moves, (3, 0, -6, 1), (-3, 1, 7, 1)), 1, both)
+    sent_x3 = send_known(coef[3], three, ((2, -1, -5, 4), (-2, -1, 3, 4), (3, 0, -6, 1), (-3, 1, 7, 1)), 1, both)
     left(sent_b2)
     left(sent_c3)
-
-    arrived(sent_b3)
-
-    def write_right(row, columns, value):
-        right[3][three.ox - 1 + row, columns, :] = value
-
-    unpack(lambda part, row: gat_b[part, row], write_right)
-    sent_r3 = send_known(right[3], three, moves)
     arrived(sent_x3)
     for row in range(-3, 4):
         for field in (0, 1):
@@ -417,8 +413,8 @@
     sent_c4 = send_known(coef[4], four, ((3, -3, -6, 3), (-3, 1, 4, 3)), 1, both)
     weights(three)
     left(sent_x3)
-    left(sent_b3)
-    arrived(sent_r3)
+    own_b3.wait()
+    arrived(sent_b3)
     first_sweep(three)
     sweep(three, one[3], two[3], three.reach - 1)
     residual(three, 2, three.core)
@@ -435,7 +431,7 @@
             coef[5][field, five.ox + row, five.own_y, :] = value
     sent_c5 = send_known(coef[5], five, ((4, -2, -6, 4), (-4, -1, 3, 4)), 2, both)
     weights(four)
-    left(sent_r3)
+    left(sent_b3)
     left(sent_c4)
     arrived(sent_r4)
     first_sweep(four)
@@ -480,23 +476,24 @@
         value = two[2][two_.ox - 2 + i, pl.ds(two_.oy - 2, two_.columns + 4), :]
         lift(value, one_, one_.ox - 4 + 2 * i, one_.oy - 4, two_.columns + 4)
 
-    loop(two_.rows + 4, lift_one)
+    loop(two_.rows + 4, lift_one, True)
     ascend(one_, 1)
 
     def lift_zero(i):
         value = two[1][one_.ox - 1 + i, pl.ds(one_.oy - 1, one_.columns + 2), :]
         lift(value, zero, zero.ox - 2 + 2 * i, zero.oy - 2, one_.columns + 2)
 
-    loop(one_.rows + 2, lift_zero)
+    loop(one_.rows + 2, lift_zero, True)
     sweep(zero, two[0], tri[0], 1)
     y, cy = zero.core
     part = zero.rows // 4
     copies = []
     for chunk in range(4):
         x = zero.ox + chunk * part
-        here = (pl.ds(x, part), pl.ds(y, cy), slice(None))
-        centre = tri[0][here]
-        two[0][here] = 0.2 * centre + pulled(zero, tri[0], x, part, y, cy, centre)
+        for row in range(x, x + part, 2):
+            here = (pl.ds(row, 2), pl.ds(y, cy), slice(None))
+            centre = tri[0][here]
+            two[0][here] = 0.2 * centre + pulled(zero, tri[0], row, 2, y, cy, centre)
         copy = pltpu.make_async_copy(
             two[0].at[pl.ds(x, part), pl.ds(y, cy)], out_ref.at[pl.ds(chunk * part, part)], local_sem.at[chunk]
         )
@@ -509,10 +506,10 @@
 def build(mesh, rows, columns):
     gx_count, gy_count = mesh.shape["gx"], mesh.shape["gy"]
     levels = [
-        Level(0, rows, columns, False, 5),
-        Level(1, rows // 2, columns // 2, False, 7),
+        Level(0, rows, columns, False, 2),
+        Level(1, rows // 2, columns // 2, False, 3),
         Level(2, rows // 4, columns // 4, False, 12),
-        Level(3, rows // 8, columns // 8 * gy_count, True, 6),
+        Level(3, rows // 8, columns // 8 * gy_count, True, 4),
         Level(4, rows // 16, columns // 16 * gy_count, True, 11),
         Level(5, 1, columns // 32 * gy_count, True, 11),
     ]
@@ -525,8 +522,8 @@
     for _ in range(5):
         scratch += [pltpu.VMEM(level.shape(), F32) for level in levels]
     scratch += [
-        pltpu.VMEM((gy_count, 2, 4, 4, 128), F32),
-        pltpu.VMEM((gy_count, 4, 4, 128), F32),
+        pltpu.VMEM((2, 4, 4, 128), F32),
+        pltpu.VMEM((4, 4, 128), F32),
         pltpu.SMEM((TYPES,), F32),
         pltpu.SMEM((TYPES,), F32),
         pltpu.SemaphoreType.DMA((4,)),

time: 59.4 us -> 56.2 us (0.946); the launches traced: 59.3 us -> 55.1 us
  Pallas kernels: 57.6 us -> 53.4 us
    pallas_call x1, Pallas kernels: 57.6 us -> 53.4 us  [body(): return call(source, tissue, diffusivity, uptake)]
where the time goes in v4:
time: 56.2 us; the launch traced here: 55.1 us
  Pallas kernels  53.4 us (95%)
  local copies, waits for them, and re-layouts  1.67 us (3%)
    pallas_call x1, Pallas kernels, body(): return call(source, tissue, diffusivity, uptake)  53.4 us
    unnamed x1, local copies, waits for them, and re-layouts  1.67 us

profile of v4, /device:TPU:1, one launch (start us, length us, event | category | flops | bytes accessed | tf_op | source)
XLA Modules:
  0.0 55.1 jit_solution(9103441263214192500)
XLA Ops:
  0.0 53.4 %vcycle.1 = f32[16,32,128]{2,1,0:T(8,128)} custom-call(f32[16,32,128]{2,1,0:T(8,128)} %src_ref.1, s32[16,32,128]{2,1,0:T(8,128)} %tis_ref.1, f32[8]{0:T(128)} %dif_ref.1, f32[8]{0:T(128)} %upt_ref.1), custom_call_target="tpu_custom_call" | custom-call | tf_op jit(solution)/shard_map/vcycle/pallas_call | solution.py:554
  53.4 1.7 %copy.6 = f32[16,32,128]{2,1,0:T(8,128)} copy(f32[16,32,128]{2,1,0:T(8,128)} %vcycle.1) | data formatting | bytes 524288

commit v5 on v4

--- a/solution.py
+++ b/solution.py
@@ -297,7 +297,7 @@
     zero, one_, two_, three, four, five = levels
 
     barrier = pltpu.get_barrier_semaphore()
-    greeted = around(zero, zero.reach + 1) + ([(0, 2), (0, -2)] if gy_count > 4 else [])
+    greeted = around(two_, two_.reach + 1) + ([(0, 2), (0, -2), (0, 3), (0, -3)] if gy_count > 6 else [])
     for dx, dy in greeted:
         pl.semaphore_signal(barrier, inc=1, device_id=device(dx, dy), device_id_type=MESH)
     loads = []
@@ -344,6 +344,8 @@
     coarsen(zero, one_, 0)
     both = (slice(None),)
     sent_c1 = send_block(coef[1], one_, one_.reach + 1, both)
+    coarsen(one_, two_, 0)
+    sent_c2 = send_block(coef[2], two_, two_.reach + 1, both)
     weights(zero, (zero.ox + 1, (zero.rows - 2) // 2, 2), zero.core, True)
 
     arrived(sent_tis)
@@ -371,11 +373,15 @@
     sent_b1 = send_block(right[1], one_, one_.reach)
     left(sent_tis)
     left(sent_src)
+    arrived(sent_c2)
+    for field in (0, 1):
+        for row in range(4):
+            gat_c[field, row] = mean(coef[2], (field,), two_.ox - 2 + 2 * row, two_.oy, 4)
+    own_c3, sent_c3 = send_columns(gat_c, coef[3], three, ((0, -1),), 0, both)
     arrived(sent_c1)
-    coarsen(one_, two_, 2)
-    sent_c2 = send_block(coef[2], two_, two_.reach + 1, both, 2)
     weights(one_)
     left(sent_c1)
+    left(sent_c2)
 
     arrived(sent_b1)
     first_sweep(one_)
@@ -383,13 +389,11 @@
     residual(one_, 2, one_.mid)
     restrict_to(one_, two_, 1)
     sent_b2 = send_block(right[2], two_, two_.reach, (), 1)
-    arrived(sent_c2)
-    for field in (0, 1):
-        for row in range(4):
-            gat_c[field, row] = mean(coef[2], (field,), two_.ox - 2 + 2 * row, two_.oy, 4)
-    own_c3, sent_c3 = send_columns(gat_c, coef[3], three, ((0, -1),), 0, both)
+    own_c3.wait()
+    arrived(sent_c3)
+    sent_x3 = send_known(coef[3], three, ((2, -1, -5, 4), (-2, -1, 3, 4), (3, 0, -6, 1), (-3, 1, 7, 1)), 1, both)
     weights(two_)
-    left(sent_c2)
+    left(sent_c3)
     left(sent_b1)
 
     arrived(sent_b2)
@@ -400,11 +404,7 @@
         gat_b[row] = mean(tri[2], (), two_.ox - 2 + 2 * row, two_.oy, 4)
 
     own_b3, sent_b3 = send_columns(gat_b, right[3], three, ((2, -5), (-2, 3), (0, -1)), 1)
-    own_c3.wait()
-    arrived(sent_c3)
-    sent_x3 = send_known(coef[3], three, ((2, -1, -5, 4), (-2, -1, 3, 4), (3, 0, -6, 1), (-3, 1, 7, 1)), 1, both)
     left(sent_b2)
-    left(sent_c3)
     arrived(sent_x3)
     for row in range(-3, 4):
         for field in (0, 1):
@@ -514,7 +514,7 @@
         Level(5, 1, columns // 32 * gy_count, True, 11),
     ]
     zero = levels[0]
-    messages = 96
+    messages = 112
     scratch = [pltpu.VMEM(zero.shape(), jnp.int32)]
     scratch += [pltpu.VMEM(level.shape(2), F32) for level in levels]
     scratch += [pltpu.VMEM(level.shape(), F32) for level in levels]

time: 56.2 us -> 58 us (1.032)
  the two profiles are of different devices: /device:TPU:1 before, /device:TPU:65 now
where the time goes in v5:
time: 58 us; the launch traced here: 57.9 us
  Pallas kernels  56.2 us (97%)
  local copies, waits for them, and re-layouts  1.67 us (3%)
    pallas_call x1, Pallas kernels, body(): return call(source, tissue, diffusivity, uptake)  56.2 us
    unnamed x1, local copies, waits for them, and re-layouts  1.67 us

profile of v5, /device:TPU:65, one launch (start us, length us, event | category | flops | bytes accessed | tf_op | source)
XLA Modules:
  0.0 57.9 jit_solution(6313252665348985537)
XLA Ops:
  0.0 56.2 %vcycle.1 = f32[16,32,128]{2,1,0:T(8,128)} custom-call(f32[16,32,128]{2,1,0:T(8,128)} %src_ref.1, s32[16,32,128]{2,1,0:T(8,128)} %tis_ref.1, f32[8]{0:T(128)} %dif_ref.1, f32[8]{0:T(128)} %upt_ref.1), custom_call_target="tpu_custom_call" | custom-call | tf_op jit(solution)/shard_map/vcycle/pallas_call | solution.py:554
  56.2 1.7 %copy.6 = f32[16,32,128]{2,1,0:T(8,128)} copy(f32[16,32,128]{2,1,0:T(8,128)} %vcycle.1) | data formatting | bytes 524288

commit v6 on v5

--- a/solution.py
+++ b/solution.py
@@ -54,7 +54,7 @@
     return low + step * size, low, high - low
 
 
-def kernel(sizes, levels, src_ref, tis_ref, dif_ref, upt_ref, out_ref, *scratch):
+def kernel(sizes, levels, src_ref, tis_ref, types_ref, out_ref, *scratch):
     gx_count, gy_count = sizes
     names = iter(scratch)
     tis = next(names)
@@ -67,7 +67,7 @@
     two = [next(names) for _ in levels]
     tri = [next(names) for _ in levels]
     gat_c, gat_b = next(names), next(names)
-    dif, upt = next(names), next(names)
+    table = next(names)
     local_sem, send_sem, recv_sem = next(names), next(names), next(names)
 
     gx = lax.axis_index("gx")
@@ -171,12 +171,12 @@
 
     def types(x, blk, y, cy):
         kind = tis[pl.ds(x, blk), pl.ds(y, cy), :]
-        kappa = jnp.full(kind.shape, dif[0], F32)
-        sigma = jnp.full(kind.shape, upt[0], F32)
+        kappa = jnp.full(kind.shape, table[0], F32)
+        sigma = jnp.full(kind.shape, table[TYPES], F32)
         for index in range(1, TYPES):
             hit = kind == index
-            kappa = jnp.where(hit, dif[index], kappa)
-            sigma = jnp.where(hit, upt[index], sigma)
+            kappa = jnp.where(hit, table[index], kappa)
+            sigma = jnp.where(hit, table[TYPES + index], sigma)
         coef[0][0, pl.ds(x, blk), pl.ds(y, cy), :] = kappa
         coef[0][1, pl.ds(x, blk), pl.ds(y, cy), :] = sigma
 
@@ -300,22 +300,21 @@
     greeted = around(two_, two_.reach + 1) + ([(0, 2), (0, -2), (0, 3), (0, -3)] if gy_count > 6 else [])
     for dx, dy in greeted:
         pl.semaphore_signal(barrier, inc=1, device_id=device(dx, dy), device_id_type=MESH)
+    pl.semaphore_wait(barrier, len(greeted))
+
+    sent_tis = send_block(tis, zero, zero.reach + 1, (), 0, tis_ref)
+    sent_src = send_block(right[0], zero, zero.reach, (), 0, src_ref)
     loads = []
     for position, (source, target) in enumerate(
         (
             (tis_ref, tis.at[zero.own_x, zero.own_y]),
             (src_ref, right[0].at[zero.own_x, zero.own_y]),
-            (dif_ref, dif),
-            (upt_ref, upt),
+            (types_ref, table),
         )
     ):
         copy = pltpu.make_async_copy(source, target, local_sem.at[position])
         copy.start()
         loads.append(copy)
-    pl.semaphore_wait(barrier, len(greeted))
-
-    sent_tis = send_block(tis, zero, zero.reach + 1, (), 0, tis_ref)
-    sent_src = send_block(right[0], zero, zero.reach, (), 0, src_ref)
     for level in (three, four, five):
         index = level.index
         for ref in (coef[index].at[0], one[index], two[index], tri[index]):
@@ -486,21 +485,10 @@
     loop(one_.rows + 2, lift_zero, True)
     sweep(zero, two[0], tri[0], 1)
     y, cy = zero.core
-    part = zero.rows // 4
-    copies = []
-    for chunk in range(4):
-        x = zero.ox + chunk * part
-        for row in range(x, x + part, 2):
-            here = (pl.ds(row, 2), pl.ds(y, cy), slice(None))
-            centre = tri[0][here]
-            two[0][here] = 0.2 * centre + pulled(zero, tri[0], row, 2, y, cy, centre)
-        copy = pltpu.make_async_copy(
-            two[0].at[pl.ds(x, part), pl.ds(y, cy)], out_ref.at[pl.ds(chunk * part, part)], local_sem.at[chunk]
-        )
-        copy.start()
-        copies.append(copy)
-    for copy in copies:
-        copy.wait()
+    for row in range(0, zero.rows, 2):
+        here = (pl.ds(zero.ox + row, 2), pl.ds(y, cy), slice(None))
+        centre = tri[0][here]
+        out_ref[pl.ds(row, 2)] = 0.2 * centre + pulled(zero, tri[0], zero.ox + row, 2, y, cy, centre)
 
 
 def build(mesh, rows, columns):
@@ -524,8 +512,7 @@
     scratch += [
         pltpu.VMEM((2, 4, 4, 128), F32),
         pltpu.VMEM((4, 4, 128), F32),
-        pltpu.SMEM((TYPES,), F32),
-        pltpu.SMEM((TYPES,), F32),
+        pltpu.SMEM((2 * TYPES,), F32),
         pltpu.SemaphoreType.DMA((4,)),
         pltpu.SemaphoreType.DMA((messages,)),
         pltpu.SemaphoreType.DMA((messages,)),
@@ -537,13 +524,12 @@
             pl.BlockSpec(memory_space=pltpu.HBM),
             pl.BlockSpec(memory_space=pltpu.HBM),
             pl.BlockSpec(memory_space=pltpu.HBM),
-            pl.BlockSpec(memory_space=pltpu.HBM),
         ],
-        out_specs=pl.BlockSpec(memory_space=pltpu.HBM),
+        out_specs=pl.BlockSpec(memory_space=pltpu.VMEM),
         scratch_shapes=scratch,
         name="vcycle",
         compiler_params=pltpu.CompilerParams(
-            collective_id=0, has_side_effects=True, vmem_limit_bytes=64 * 2**20
+            collective_id=0, has_side_effects=True, vmem_limit_bytes=56_250_000
         ),
     )
 
@@ -551,7 +537,7 @@
 def solution(mesh):
     def body(source, tissue, diffusivity, uptake):
         call = build(mesh, source.shape[0], source.shape[1])
-        return call(source, tissue, diffusivity, uptake)
+        return call(source, tissue, jnp.concatenate([diffusivity, uptake]))
 
     in_specs = (P("gx", "gy", None), P("gx", "gy", None), P(), P())
     out_specs = P("gx", "gy", None)

time: 58 us -> 57.5 us (level)
  local copies, waits for them, and re-layouts: 1.67 us -> 0.71 us
  other arithmetic: 0 us -> 0.75 us
    unnamed x1, local copies, waits for them, and re-layouts: 1.67 us -> 0.71 us
    concatenate x0 -> x1, other arithmetic: none -> 0.75 us  [body(): return call(source, tissue, jnp.concatenate([diffusivity, uptake]))]
where the time goes in v6:
time: 57.5 us; the launch traced here: 57.3 us
  Pallas kernels  55.9 us (97%)
  other arithmetic  0.75 us (1%)
  local copies, waits for them, and re-layouts  0.71 us (1%)
    pallas_call x1, Pallas kernels, body(): return call(source, tissue, jnp.concatenate([diffusivity, uptake]))  55.9 us

profile of v6, /device:TPU:65, one launch (start us, length us, event | category | flops | bytes accessed | tf_op | source)
XLA Modules:
  0.0 57.3 jit_solution(17424987385764558175)
XLA Ops:
  0.0 0.7 %pad_maximum_fusion.types_ref = f32[16]{0:T(128)S(1)} fusion(f32[8]{0:T(128)} %param.7, f32[8]{0:T(128)} %param.6), kind=kLoop, calls=%fused_computation | loop fusion | flops 16 | bytes 128 | tf_op jit(solution)/shard_map/concatenate | solution.py:540
  0.7 55.9 %vcycle.1 = f32[16,32,128]{2,1,0:T(8,128)S(1)} custom-call(f32[16,32,128]{2,1,0:T(8,128)} %src_ref.1, s32[16,32,128]{2,1,0:T(8,128)} %tis_ref.1, f32[16]{0:T(128)S(1)} %pad_maximum_fusion.types_ref), custom_call_target="tpu_custom_call" | custom-call | tf_op jit(solution)/shard_map/vcycle/pallas_call | solution.py:540
  56.6 0.7 %copy.6 = f32[16,32,128]{2,1,0:T(8,128)} copy(f32[16,32,128]{2,1,0:T(8,128)S(1)} %vcycle.1) | data formatting | bytes 524288

commit v7 on v6

--- a/solution.py
+++ b/solution.py
@@ -297,7 +297,7 @@
     zero, one_, two_, three, four, five = levels
 
     barrier = pltpu.get_barrier_semaphore()
-    greeted = around(two_, two_.reach + 1) + ([(0, 2), (0, -2), (0, 3), (0, -3)] if gy_count > 6 else [])
+    greeted = around(zero, zero.reach + 1) + ([(0, 2), (0, -2)] if gy_count > 4 else [])
     for dx, dy in greeted:
         pl.semaphore_signal(barrier, inc=1, device_id=device(dx, dy), device_id_type=MESH)
     pl.semaphore_wait(barrier, len(greeted))
@@ -343,8 +343,6 @@
     coarsen(zero, one_, 0)
     both = (slice(None),)
     sent_c1 = send_block(coef[1], one_, one_.reach + 1, both)
-    coarsen(one_, two_, 0)
-    sent_c2 = send_block(coef[2], two_, two_.reach + 1, both)
     weights(zero, (zero.ox + 1, (zero.rows - 2) // 2, 2), zero.core, True)
 
     arrived(sent_tis)
@@ -372,15 +370,11 @@
     sent_b1 = send_block(right[1], one_, one_.reach)
     left(sent_tis)
     left(sent_src)
-    arrived(sent_c2)
-    for field in (0, 1):
-        for row in range(4):
-            gat_c[field, row] = mean(coef[2], (field,), two_.ox - 2 + 2 * row, two_.oy, 4)
-    own_c3, sent_c3 = send_columns(gat_c, coef[3], three, ((0, -1),), 0, both)
     arrived(sent_c1)
+    coarsen(one_, two_, 2)
+    sent_c2 = send_block(coef[2], two_, two_.reach + 1, both, 2)
     weights(one_)
     left(sent_c1)
-    left(sent_c2)
 
     arrived(sent_b1)
     first_sweep(one_)
@@ -388,11 +382,13 @@
     residual(one_, 2, one_.mid)
     restrict_to(one_, two_, 1)
     sent_b2 = send_block(right[2], two_, two_.reach, (), 1)
-    own_c3.wait()
-    arrived(sent_c3)
-    sent_x3 = send_known(coef[3], three, ((2, -1, -5, 4), (-2, -1, 3, 4), (3, 0, -6, 1), (-3, 1, 7, 1)), 1, both)
+    arrived(sent_c2)
+    for field in (0, 1):
+        for row in range(4):
+            gat_c[field, row] = mean(coef[2], (field,), two_.ox - 2 + 2 * row, two_.oy, 4)
+    own_c3, sent_c3 = send_columns(gat_c, coef[3], three, ((0, -1),), 0, both)
     weights(two_)
-    left(sent_c3)
+    left(sent_c2)
     left(sent_b1)
 
     arrived(sent_b2)
@@ -403,7 +399,11 @@
         gat_b[row] = mean(tri[2], (), two_.ox - 2 + 2 * row, two_.oy, 4)
 
     own_b3, sent_b3 = send_columns(gat_b, right[3], three, ((2, -5), (-2, 3), (0, -1)), 1)
+    own_c3.wait()
+    arrived(sent_c3)
+    sent_x3 = send_known(coef[3], three, ((2, -1, -5, 4), (-2, -1, 3, 4), (3, 0, -6, 1), (-3, 1, 7, 1)), 1, both)
     left(sent_b2)
+    left(sent_c3)
     arrived(sent_x3)
     for row in range(-3, 4):
         for field in (0, 1):
@@ -502,7 +502,7 @@
         Level(5, 1, columns // 32 * gy_count, True, 11),
     ]
     zero = levels[0]
-    messages = 112
+    messages = 96
     scratch = [pltpu.VMEM(zero.shape(), jnp.int32)]
     scratch += [pltpu.VMEM(level.shape(2), F32) for level in levels]
     scratch += [pltpu.VMEM(level.shape(), F32) for level in levels]

time: 57.5 us -> 55.8 us (0.970)
  the two profiles are of different devices: /device:TPU:65 before, /device:TPU:1 now
where the time goes in v7:
time: 55.8 us; the launch traced here: 55.1 us
  Pallas kernels  53.6 us (96%)
  other arithmetic  0.75 us (1%)
  local copies, waits for them, and re-layouts  0.71 us (1%)
    pallas_call x1, Pallas kernels, body(): return call(source, tissue, jnp.concatenate([diffusivity, uptake]))  53.6 us

profile of v7, /device:TPU:1, one launch (start us, length us, event | category | flops | bytes accessed | tf_op | source)
XLA Modules:
  0.0 55.1 jit_solution(11703941246456942658)
XLA Ops:
  0.0 0.7 %pad_maximum_fusion.types_ref = f32[16]{0:T(128)S(1)} fusion(f32[8]{0:T(128)} %param.7, f32[8]{0:T(128)} %param.6), kind=kLoop, calls=%fused_computation | loop fusion | flops 16 | bytes 128 | tf_op jit(solution)/shard_map/concatenate | solution.py:540
  0.7 53.6 %vcycle.1 = f32[16,32,128]{2,1,0:T(8,128)S(1)} custom-call(f32[16,32,128]{2,1,0:T(8,128)} %src_ref.1, s32[16,32,128]{2,1,0:T(8,128)} %tis_ref.1, f32[16]{0:T(128)S(1)} %pad_maximum_fusion.types_ref), custom_call_target="tpu_custom_call" | custom-call | tf_op jit(solution)/shard_map/vcycle/pallas_call | solution.py:540
  54.4 0.7 %copy.6 = f32[16,32,128]{2,1,0:T(8,128)} copy(f32[16,32,128]{2,1,0:T(8,128)S(1)} %vcycle.1) | data formatting | bytes 524288

commit v8 on v7

--- a/solution.py
+++ b/solution.py
@@ -392,6 +392,10 @@
     left(sent_b1)
 
     arrived(sent_b2)
+    own_c3.wait()
+    arrived(sent_c3)
+    sent_x3 = send_known(coef[3], three, ((2, -1, -5, 4), (-2, -1, 3, 4)), 1, both)
+    sent_x3 = sent_x3 + send_known(coef[3], three, ((3, 0, -6, 1), (-3, 1, 7, 1)), 1, both)
     first_sweep(two_)
     sweep(two_, one[2], two[2], two_.reach - 1)
     residual(two_, 2, two_.core)
@@ -399,9 +403,6 @@
         gat_b[row] = mean(tri[2], (), two_.ox - 2 + 2 * row, two_.oy, 4)
 
     own_b3, sent_b3 = send_columns(gat_b, right[3], three, ((2, -5), (-2, 3), (0, -1)), 1)
-    own_c3.wait()
-    arrived(sent_c3)
-    sent_x3 = send_known(coef[3], three, ((2, -1, -5, 4), (-2, -1, 3, 4), (3, 0, -6, 1), (-3, 1, 7, 1)), 1, both)
     left(sent_b2)
     left(sent_c3)
     arrived(sent_x3)

time: 55.8 us -> 57 us (1.022)
  the two profiles are of different devices: /device:TPU:1 before, /device:TPU:113 now
where the time goes in v8:
time: 57 us; the launch traced here: 56.8 us
  Pallas kernels  55.4 us (97%)
  other arithmetic  0.75 us (1%)
  local copies, waits for them, and re-layouts  0.71 us (1%)
    pallas_call x1, Pallas kernels, body(): return call(source, tissue, jnp.concatenate([diffusivity, uptake]))  55.4 us

profile of v8, /device:TPU:113, one launch (start us, length us, event | category | flops | bytes accessed | tf_op | source)
XLA Modules:
  0.0 56.8 jit_solution(185155492888486144)
XLA Ops:
  0.0 0.7 %pad_maximum_fusion.types_ref = f32[16]{0:T(128)S(1)} fusion(f32[8]{0:T(128)} %param.7, f32[8]{0:T(128)} %param.6), kind=kLoop, calls=%fused_computation | loop fusion | flops 16 | bytes 128 | tf_op jit(solution)/shard_map/concatenate | solution.py:541
  0.7 55.4 %vcycle.1 = f32[16,32,128]{2,1,0:T(8,128)S(1)} custom-call(f32[16,32,128]{2,1,0:T(8,128)} %src_ref.1, s32[16,32,128]{2,1,0:T(8,128)} %tis_ref.1, f32[16]{0:T(128)S(1)} %pad_maximum_fusion.types_ref), custom_call_target="tpu_custom_call" | custom-call | tf_op jit(solution)/shard_map/vcycle/pallas_call | solution.py:541
  56.1 0.7 %copy.6 = f32[16,32,128]{2,1,0:T(8,128)} copy(f32[16,32,128]{2,1,0:T(8,128)S(1)} %vcycle.1) | data formatting | bytes 524288
